TPU v7x, 512 devices: a whole 4x4x16 slice. The times are simulated.
512 devices in a mesh: fsdp: 32 (over z, x_hi), seq: 16 (over y, x_lo, core).
Axes of the slice: x: 4 (x_hi: 2, x_lo: 2; x = x_hi * 2 + x_lo), y: 4, z: 16, core: 2. Of those that a mesh axis runs over, the one named last changes fastest.
Arguments:
- queries: bfloat16 [32, 16, 128, 2560], P('fsdp', 'seq'), may hold values from -60 to 60
- keys: bfloat16 [32, 16, 128, 2560], P('fsdp', 'seq'), may hold values from -60 to 60
- values: bfloat16 [32, 16, 128, 2560], P('fsdp', 'seq'), may hold values from -6 to 6
- grad_out: bfloat16 [32, 16, 128, 2560], P('fsdp', 'seq'), may hold values from -6 to 6
- q_gain: float32 [2560], P('fsdp'), may hold values from 0.5 to 1.5
- k_gain: float32 [2560], P('fsdp'), may hold values from 0.5 to 1.5
- lengths: int32 [32], P('fsdp'), may hold values from 1 to 16, as said below
- windows: int32 [20, 3], replicated, may hold values from 0 to 1, as said below
Outputs:
- d_queries: bfloat16 [32, 16, 128, 2560], P('fsdp', 'seq')
- d_keys: bfloat16 [32, 16, 128, 2560], P('fsdp', 'seq')
- d_values: bfloat16 [32, 16, 128, 2560], P('fsdp', 'seq')
- d_q_gain: float32 [2560], P('fsdp')
- d_k_gain: float32 [2560], P('fsdp')
Inputs may be any that keep to these rules, and one draw needn't show every extreme that they name: `lengths`: some clip has all 16 frames. `windows`: frame half-widths reach 1 in some head; tile half-widths are 0 or 1.
All inputs are finite; a program needn't handle non-finite values.
Results may differ from a plain program's by a relative error of at most 0.012.
The roundings to bfloat16 on the way count: a program that leaves them out, or rounds other values in their place, can miss the bound.
Values may be sent and summed in bfloat16 or wider, within the bound.
A program may use at most 128 MiB of HBM per device.

v0:
```python
import jax
import jax.numpy as jnp
from jax import lax
from jax.sharding import PartitionSpec as P

PW = 8
TILE_H = 4
TILE_W = 4


def padded(block, sides, width):
    for axis, dim in sides:
        count = lax.axis_size(axis)
        forward = [(i, i + 1) for i in range(count - 1)]
        backward = [(target, source) for source, target in forward]
        low = lax.ppermute(
            lax.slice_in_dim(block, block.shape[dim] - width, None, axis=dim), axis, forward
        )
        high = lax.ppermute(lax.slice_in_dim(block, 0, width, axis=dim), axis, backward)
        block = jnp.concatenate([low, block, high], axis=dim)
    return block


def shifted(value, axis, steps):
    count = lax.axis_size(axis)
    first, last = (max(0, -steps), min(count, count - steps))
    return lax.ppermute(value, axis, [(source, source + steps) for source in range(first, last)])


def positions(first_frame, frame_count, pixels):
    row_index = jnp.arange(frame_count * pixels, dtype=jnp.int32)
    frame_of = first_frame + row_index // pixels
    pixel_of = row_index % pixels
    return (frame_of, pixel_of // PW // TILE_H, pixel_of % PW // TILE_W)


def within_reach(left, right, limit):
    return jnp.abs(left[:, None] - right[None, :])[None] <= limit[:, None, None]


def window_mask(query_pos, key_pos, windows, length):
    inside = within_reach(query_pos[0], key_pos[0], windows[:, 0])
    inside = inside & within_reach(query_pos[1], key_pos[1], windows[:, 1])
    inside = inside & within_reach(query_pos[2], key_pos[2], windows[:, 2])
    key_valid = (key_pos[0] >= 0) & (key_pos[0] < length)
    query_valid = (query_pos[0] >= 0) & (query_pos[0] < length)
    return inside & key_valid[None, None, :] & query_valid[None, :, None]


def contract(form, left, right):
    return jnp.einsum(form, left, right, preferred_element_type=jnp.float32)


def query_side(query_normed, key_normed, value_rows, upstream, allowed, factor):
    scores = contract("qhd,khd->hqk", query_normed, key_normed) * factor
    summit = jnp.max(jnp.where(allowed, scores, -1e30), -1)
    alive = jnp.any(allowed, -1)
    summit = jnp.where(alive, summit, 0.0)
    totals = jnp.sum(jnp.where(allowed, jnp.exp(scores - summit[..., None]), 0.0), -1)
    totals = totals + jnp.where(alive, 0.0, 1.0)
    logsum = summit + jnp.log(totals)
    probs = jnp.where(allowed, jnp.exp(scores - logsum[..., None]), 0.0)
    weights = probs.astype(jnp.bfloat16)
    attended = contract("hqk,khd->qhd", weights, value_rows)
    deltas = jnp.sum(upstream.astype(jnp.float32) * attended, -1)
    dprobs = contract("qhd,khd->hqk", upstream, value_rows)
    dscores = (probs * (dprobs - deltas.T[:, :, None])).astype(jnp.bfloat16)
    query_grad = contract("hqk,khd->qhd", dscores, key_normed) * factor
    return (logsum.T, deltas, query_grad, weights, dscores)


def normed(row_data, gain_vec):
    widened = row_data.astype(jnp.float32)
    inverse = lax.rsqrt(jnp.mean(widened * widened, -1, keepdims=True) + 1e-06)
    return ((widened * inverse * gain_vec).astype(jnp.bfloat16), widened, inverse)


def norm_back(upstream, widened, inverse, gain_vec):
    scaled = upstream * gain_vec
    inner = jnp.mean(scaled * widened, -1, keepdims=True)
    grad_rows = inverse * (scaled - widened * inverse * inverse * inner)
    return (grad_rows.astype(jnp.bfloat16), jnp.sum(upstream * widened * inverse, 0))


def local(queries, keys, values, grad_out, q_gain, k_gain, lengths, windows):
    frame_count, pixels, columns = (queries.shape[1], queries.shape[2], queries.shape[3])
    head_count = windows.shape[0]
    head_size = columns // head_count
    row_count = frame_count * pixels
    factor = head_size ** (-0.5)
    query_gain_full, key_gain_full = (
        lax.all_gather(q_gain, "fsdp", axis=0, tiled=True),
        lax.all_gather(k_gain, "fsdp", axis=0, tiled=True),
    )
    query_normed, query_wide, query_inv = normed(
        queries.reshape(row_count, columns), query_gain_full
    )
    key_normed, key_wide, key_inv = normed(keys.reshape(row_count, columns), key_gain_full)
    value_rows = values.reshape(row_count, columns)
    upstream = grad_out.reshape(row_count, columns)
    length = lengths[0]
    first_frame = lax.axis_index("seq") * frame_count
    heads_view = (row_count, head_count, head_size)
    wide_view = (3 * row_count, head_count, head_size)
    stacked_keys = jnp.stack([key_normed, value_rows]).reshape(2, 1, frame_count, pixels, columns)
    key_window = padded(stacked_keys, (("seq", 2),), frame_count)
    near_keys = key_window[0].reshape(wide_view)
    near_values = key_window[1].reshape(wide_view)
    own_pos = positions(first_frame, frame_count, pixels)
    near_pos = positions(first_frame - frame_count, 3 * frame_count, pixels)
    allowed = window_mask(own_pos, near_pos, windows, length)
    query_heads = query_normed.reshape(heads_view)
    upstream_heads = upstream.reshape(heads_view)
    logsum, deltas, query_grad, weights, dscores = query_side(
        query_heads, near_keys, near_values, upstream_heads, allowed, factor
    )
    value_terms = contract("hqk,qhd->khd", weights, upstream_heads)
    key_terms = contract("hqk,qhd->khd", dscores, query_heads) * factor
    partials = jnp.stack([key_terms, value_terms]).reshape(2, 3, row_count, columns)
    from_above = shifted(partials[:, 0], "seq", -1)
    from_below = shifted(partials[:, 2], "seq", 1)
    combined = partials[:, 1] + from_above + from_below
    key_grad = combined[0]
    value_grad = combined[1]
    query_out, query_gain_grad = norm_back(
        query_grad.reshape(row_count, columns), query_wide, query_inv, query_gain_full
    )
    key_out, key_gain_grad = norm_back(key_grad, key_wide, key_inv, key_gain_full)
    value_out = value_grad.astype(jnp.bfloat16)
    gain_grads = jnp.stack([query_gain_grad, key_gain_grad])
    grouped = lax.psum(gain_grads, "seq")
    shares = lax.psum_scatter(grouped, "fsdp", scatter_dimension=1, tiled=True)
    out_shape = queries.shape
    return (
        query_out.reshape(out_shape),
        key_out.reshape(out_shape),
        value_out.reshape(out_shape),
        shares[0],
        shares[1],
    )


def solution(mesh):
    in_specs = (
        P("fsdp", "seq", None, None),
        P("fsdp", "seq", None, None),
        P("fsdp", "seq", None, None),
        P("fsdp", "seq", None, None),
        P("fsdp"),
        P("fsdp"),
        P("fsdp"),
        P(),
    )
    out_specs = (
        P("fsdp", "seq", None, None),
        P("fsdp", "seq", None, None),
        P("fsdp", "seq", None, None),
        P("fsdp"),
        P("fsdp"),
    )
    return jax.shard_map(local, mesh=mesh, in_specs=in_specs, out_specs=out_specs, check_vma=False)
```

profile of v0, /device:TPU:1, one launch (start us, length us, event | category | flops | bytes accessed | tf_op | source)
XLA Modules:
  0.0 1027.7 jit_solution(7309665369162974773)
XLA Ops:
  12.3 127.3 %all-reduce.2 = (f32[2560]{0:T(1024)S(1)}, f32[2560]{0:T(1024)S(1)}) all-reduce(f32[2560]{0:T(1024)S(1)} %dynamic-update-slice, f32[2560]{0:T(1024)S(1)} %dynamic-update-slice.1), channel_id=1, replica_groups=mesh['fsdp'=32,'seq'=16] {'fsdp'}, use_global_device_ids=true, to_apply=%add | all-reduce | flops 5120 | bytes 40960
  142.1 30.5 %collective-permute-start.1 = (bf16[2,1,1,128,2560]{4,3,0,2,1:T(8,128)(2,1)S(1)}, bf16[2,1,1,128,2560]{4,3,0,2,1:T(8,128)(2,1)}, u32[]{:S(2)}, u32[]{:S(2)}) collective-permute-start(bf16[2,1,1,128,2560]{4,3,0,2,1:T(8,128)(2,1)S(1)} %maximum_bitcast_fusion), channel_id=1, source_target_pairs={{1,0},{2,1},{3,2},{4,3},{5,4},{6,5},{7,6},{8,7},{9,8},{10,9},{11,1... | collective-permute-start | bytes 3932168 | tf_op jit(solution)/shard_map/ppermute | solution.py:19
  172.5 2.1 collective-permute-start
  175.9 2.2 copy.43
  179.6 18.6 %collective-permute-done.1 = bf16[2,1,1,128,2560]{4,3,0,2,1:T(8,128)(2,1)} collective-permute-done((bf16[2,1,1,128,2560]{4,3,0,2,1:T(8,128)(2,1)S(1)}, bf16[2,1,1,128,2560]{4,3,0,2,1:T(8,128)(2,1)}, u32[]{:S(2)}, u32[]{:S(2)}) %collective-permute-start.1) | collective-permute-done | bytes 1310752 | tf_op jit(solution)/shard_map/ppermute | solution.py:19
  198.2 2.1 pad_maximum_fusion
  200.4 1.5 fusion.48
  201.9 4.3 reshape_squeeze.7
  206.2 4.3 copy.46
  210.5 2.6 reshape_squeeze.6
  213.1 3.2 copy.48
  216.3 3.4 select_reduce_fusion.1
  219.8 2.4 select_reduce_fusion
  222.2 2.4 convolution_bitcast_fusion
  224.7 2.6 fusion.28
  227.3 3.0 fusion
  230.3 2.7 multiply_bitcast_fusion
  233.0 4.4 copy.53
  237.4 5.0 stack.24
  242.4 7.0 reshape.585
  249.4 6.6 copy.61
  256.0 5.2 fusion.2
  261.3 1.9 collective-permute-start.2
  263.2 3.6 collective-permute-start.3
  266.9 2.4 broadcast_multiply_fusion
  269.3 1.8 copy.49
  271.1 2.2 fusion.27
  274.6 41.2 %collective-permute-done.2 = f32[2,128,2560]{2,1,0:T(8,128)} collective-permute-done((f32[2,128,2560]{2,1,0:T(8,128)}, f32[2,128,2560]{2,1,0:T(8,128)}, u32[]{:S(2)}, u32[]{:S(2)}) %collective-permute-start.2) | collective-permute-done | bytes 2621472 | tf_op jit(solution)/shard_map/ppermute | solution.py:27
  315.9 3.5 fusion.6
  321.1 1.5 copy.62
  323.6 657.5 %reduce-scatter.4.cloned.1.call-done = f32[80,2]{1,0:T(8,128)} async-done(((f32[2560,2]{1,0:T(8,128)}), f32[80,2]{1,0:T(8,128)}) %reduce-scatter.4.cloned.1.call-update) | async-done | bytes 656
  981.9 38.4 %psum.8 = f32[2,80]{1,0:T(2,128)S(1)} all-reduce(f32[2,80]{1,0:T(2,128)S(1)} %copy.63), channel_id=1, replica_groups=mesh['fsdp'=32,'seq'=16] {'seq'}, use_global_device_ids=true, to_apply=%region_10.11 | all-reduce | flops 160 | bytes 1280 | tf_op jit(solution)/shard_map/psum | solution.py:131
  (68 shorter events, 14.3 us)
Async XLA Ops:
  7.2 167.5 %copy-start.4 = (bf16[1,1,128,2560]{3,2,1,0:T(8,128)(2,1)S(1)}, bf16[1,1,128,2560]{3,2,1,0:T(8,128)(2,1)}, u32[]{:S(2)}) copy-start(bf16[1,1,128,2560]{3,2,1,0:T(8,128)(2,1)} %param.8) | copy-start | bytes 1966084
  7.2 973.9 %reduce-scatter.4.cloned.1.call-start = ((), (), s32[]{:S(2)}) async-start(), calls=%async_computation.1 | async-start | bytes 1351680
  142.1 36.0 %copy-start.12 = (s32[20,3]{0,1:T(4,128)S(1)}, s32[20,3]{0,1:T(4,128)}, u32[]{:S(2)}) copy-start(s32[20,3]{0,1:T(4,128)} %param.15) | copy-start | bytes 724
  142.1 56.2 %collective-permute-start.1 = (bf16[2,1,1,128,2560]{4,3,0,2,1:T(8,128)(2,1)S(1)}, bf16[2,1,1,128,2560]{4,3,0,2,1:T(8,128)(2,1)}, u32[]{:S(2)}, u32[]{:S(2)}) collective-permute-start(bf16[2,1,1,128,2560]{4,3,0,2,1:T(8,128)(2,1)S(1)} %maximum_bitcast_fusion), channel_id=1, source_target_pairs={{1,0},{2,1},{3,2},{4,3},{5,4},{6,5},{7,6},{8,7},{9,8},{10,9},{11,1... | collective-permute-start | bytes 3932168 | tf_op jit(solution)/shard_map/ppermute | solution.py:19
  172.5 25.7 %collective-permute-start = (bf16[2,1,1,128,2560]{4,3,0,2,1:T(8,128)(2,1)S(1)}, bf16[2,1,1,128,2560]{4,3,0,2,1:T(8,128)(2,1)}, u32[]{:S(2)}, u32[]{:S(2)}) collective-permute-start(bf16[2,1,1,128,2560]{4,3,0,2,1:T(8,128)(2,1)S(1)} %maximum_bitcast_fusion), channel_id=1, source_target_pairs={{0,1},{1,2},{2,3},{3,4},{4,5},{5,6},{6,7},{7,8},{8,9},{9,10},{10,1... | collective-permute-start | bytes 3932168 | tf_op jit(solution)/shard_map/ppermute | solution.py:16
  178.3 19.9 %copy-start.7 = (s32[128,384]{1,0:T(8,128)}, s32[128,384]{1,0:T(8,128)S(1)}, u32[]{:S(2)}) copy-start(s32[128,384]{1,0:T(8,128)S(1)} %get-tuple-element.24) | copy-start | bytes 589828
  178.3 19.9 %copy-start.9 = (s32[128,384]{1,0:T(8,128)}, s32[128,384]{1,0:T(8,128)S(1)}, u32[]{:S(2)}) copy-start(s32[128,384]{1,0:T(8,128)S(1)} %get-tuple-element.25) | copy-start | bytes 589828
  216.3 3.5 copy-start.8
  216.3 3.5 copy-start.10
  219.7 2.5 copy-start.11
  222.2 2.5 copy-start.6
  230.3 2.7 copy-start.2
  256.0 10.8 %copy-start.3 = (bf16[20,128,384]{2,1,0:T(8,128)(2,1)S(1)}, bf16[20,128,384]{2,1,0:T(8,128)(2,1)}, u32[]{:S(2)}) copy-start(bf16[20,128,384]{2,1,0:T(8,128)(2,1)} %copy-done.2) | copy-start | bytes 5898244
  261.3 54.6 %collective-permute-start.2 = (f32[2,128,2560]{2,1,0:T(8,128)}, f32[2,128,2560]{2,1,0:T(8,128)}, u32[]{:S(2)}, u32[]{:S(2)}) collective-permute-start(f32[2,128,2560]{2,1,0:T(8,128)} %get-tuple-element.11), channel_id=1, source_target_pairs={{1,0},{2,1},{3,2},{4,3},{5,4},{6,5},{7,6},{8,7},{9,8},{10,9},{11,1... | collective-permute-start | bytes 7864328 | tf_op jit(solution)/shard_map/ppermute | solution.py:27
  263.2 52.7 %collective-permute-start.3 = (f32[2,128,2560]{2,1,0:T(8,128)}, f32[2,128,2560]{2,1,0:T(8,128)}, u32[]{:S(2)}, u32[]{:S(2)}) collective-permute-start(f32[2,128,2560]{2,1,0:T(8,128)} %get-tuple-element.12), channel_id=1, source_target_pairs={{0,1},{1,2},{2,3},{3,4},{4,5},{5,6},{6,7},{7,8},{8,9},{9,10},{10,1... | collective-permute-start | bytes 7864328 | tf_op jit(solution)/shard_map/ppermute | solution.py:27
  269.3 4.1 copy-start.5
  271.1 44.8 %copy-start = (f32[1,3,128,2560]{3,2,1,0:T(8,128)S(1)}, f32[1,3,128,2560]{3,2,1,0:T(8,128)}, u32[]{:S(2)}) copy-start(f32[1,3,128,2560]{3,2,1,0:T(8,128)} %stack.24) | copy-start | bytes 11796484
  274.6 44.8 %copy-start.1 = (bf16[1,1,128,2560]{3,2,1,0:T(8,128)(2,1)S(1)}, bf16[1,1,128,2560]{3,2,1,0:T(8,128)(2,1)}, u32[]{:S(2)}) copy-start(bf16[1,1,128,2560]{3,2,1,0:T(8,128)(2,1)} %param.9) | copy-start | bytes 1966084
Sparse Core Ops, SparseCore 0:
  322.8 658.2 reduce-scatter.3
where the time goes:
time: 1030 us
  waiting for transfers between devices  717 us (70%)
  blocking collectives  166 us (16%)
  local copies, waits for them, and re-layouts  50 us (5%)
  starting transfers between devices  38.1 us (4%)
  other arithmetic  24.2 us (2%)
  matrix products  16.6 us (2%)
  between operations  15.7 us (2%)
    unnamed x2, waiting for transfers between devices  657 us
    unnamed x1, blocking collectives  127 us
    ppermute x2, waiting for transfers between devices, shifted(): lax.ppermute(value, axis, [(source, source + steps) for source in range(f...  41.3 us
    psum x1, blocking collectives, local(): grouped = lax.psum(gain_grads, 'seq')  38.4 us
    ppermute x1, starting transfers between devices, padded(): lax.ppermute(lax.slice_in_dim(block, 0, width, axis=dim), axis, backward)  30.5 us
  transfers between devices with their start and end apart: 5, of which 3 were waited for; matrix products, arithmetic and copies ran while one was open for 1% of the time, Pallas kernels for 0%

commit v1 on v0

--- a/solution.py
+++ b/solution.py
@@ -1,11 +1,196 @@
 import jax
 import jax.numpy as jnp
 from jax import lax
+from jax.experimental import pallas as pl
+from jax.experimental.pallas import tpu as pltpu
 from jax.sharding import PartitionSpec as P
 
 PW = 8
 TILE_H = 4
 TILE_W = 4
+MESH = pl.DeviceIdType.MESH
+LANES = 128
+
+
+def gather_gains_kernel(count, q_ref, k_ref, out_ref, mine, inbox, send_sem, recv_sem):
+    me = lax.axis_index("fsdp")
+    width = q_ref.shape[1]
+    barrier = pltpu.get_barrier_semaphore()
+
+    def greet(step, carry):
+        peer = lax.rem(me + step, count)
+        pl.semaphore_signal(barrier, inc=1, device_id={"fsdp": peer}, device_id_type=MESH)
+        return carry
+
+    lax.fori_loop(1, count, greet, 0)
+    mine[...] = jnp.zeros_like(mine)
+    mine[0:1, 0:width] = q_ref[...]
+    mine[0:1, LANES : LANES + width] = k_ref[...]
+    inbox[pl.ds(me, 1)] = mine[...][None]
+    pl.semaphore_wait(barrier, count - 1)
+
+    def copy(step):
+        peer = lax.rem(me + step, count)
+        return pltpu.make_async_remote_copy(
+            src_ref=mine,
+            dst_ref=inbox.at[me],
+            send_sem=send_sem.at[step],
+            recv_sem=recv_sem.at[step],
+            device_id={"fsdp": peer},
+            device_id_type=MESH,
+        )
+
+    def start(step, carry):
+        copy(step).start()
+        return carry
+
+    def finish(step, carry):
+        copy(step).wait()
+        return carry
+
+    lax.fori_loop(1, count, start, 0)
+    lax.fori_loop(1, count, finish, 0)
+    lane = lax.broadcasted_iota(jnp.int32, (1, LANES), 1)
+    for row in range(2):
+        tiles = [jnp.zeros((1, LANES), jnp.float32) for _ in range(out_ref.shape[1] // LANES + 1)]
+        for owner in range(count):
+            tile, offset = divmod(owner * width, LANES)
+            part = inbox[owner, :, row * LANES : (row + 1) * LANES]
+            if offset:
+                part = pltpu.roll(part, offset, 1)
+            if offset + width > LANES:
+                tiles[tile + 1] = tiles[tile + 1] + jnp.where(lane < offset, part, 0.0)
+                part = jnp.where(lane >= offset, part, 0.0)
+            tiles[tile] = tiles[tile] + part
+        for at in range(out_ref.shape[1] // LANES):
+            out_ref[row : row + 1, at * LANES : (at + 1) * LANES] = tiles[at]
+
+
+def gather_gains(q_gain, k_gain):
+    count = lax.axis_size("fsdp")
+    width = q_gain.shape[0]
+    return pl.pallas_call(
+        lambda *refs: gather_gains_kernel(count, *refs),
+        out_shape=jax.ShapeDtypeStruct((2, count * width), jnp.float32),
+        in_specs=[pl.BlockSpec(memory_space=pltpu.VMEM)] * 2,
+        out_specs=pl.BlockSpec(memory_space=pltpu.VMEM),
+        scratch_shapes=[
+            pltpu.VMEM((1, 2 * LANES), jnp.float32),
+            pltpu.VMEM((count, 1, 2 * LANES), jnp.float32),
+            pltpu.SemaphoreType.DMA((count,)),
+            pltpu.SemaphoreType.DMA((count,)),
+        ],
+        compiler_params=pltpu.CompilerParams(collective_id=0, has_side_effects=True),
+        name="gather_gains",
+    )(q_gain[None], k_gain[None])
+
+
+def reduce_gains_kernel(
+    count, group, gains_ref, q_ref, k_ref, outbox, inbox, mine, inbox_seq, send_sem, recv_sem, send_seq, recv_seq
+):
+    me = lax.axis_index("fsdp")
+    rank = lax.axis_index("seq")
+    width = q_ref.shape[1]
+    barrier = pltpu.get_barrier_semaphore()
+
+    def greet(step, carry):
+        peer = lax.rem(me + step, count)
+        pl.semaphore_signal(barrier, inc=1, device_id={"fsdp": peer}, device_id_type=MESH)
+        return carry
+
+    def greet_seq(step, carry):
+        peer = lax.rem(rank + step, group)
+        pl.semaphore_signal(barrier, inc=1, device_id={"seq": peer}, device_id_type=MESH)
+        return carry
+
+    lax.fori_loop(1, count, greet, 0)
+    lax.fori_loop(1, group, greet_seq, 0)
+    lane = lax.broadcasted_iota(jnp.int32, (1, LANES), 1)
+    for owner in range(count):
+        tile, offset = divmod(owner * width, LANES)
+        for row in range(2):
+            part = gains_ref[row : row + 1, tile * LANES : (tile + 1) * LANES]
+            if offset:
+                part = pltpu.roll(part, LANES - offset, 1)
+            if offset + width > LANES:
+                after = gains_ref[row : row + 1, (tile + 1) * LANES : (tile + 2) * LANES]
+                after = pltpu.roll(after, LANES - offset, 1)
+                part = jnp.where(lane < LANES - offset, part, after)
+            outbox[owner, :, row * LANES : (row + 1) * LANES] = part
+    inbox[pl.ds(me, 1)] = outbox[pl.ds(me, 1)]
+    pl.semaphore_wait(barrier, count + group - 2)
+
+    def copy(step):
+        peer = lax.rem(me + step, count)
+        return pltpu.make_async_remote_copy(
+            src_ref=outbox.at[peer],
+            dst_ref=inbox.at[me],
+            send_sem=send_sem.at[step],
+            recv_sem=recv_sem.at[step],
+            device_id={"fsdp": peer},
+            device_id_type=MESH,
+        )
+
+    def copy_seq(step):
+        peer = lax.rem(rank + step, group)
+        return pltpu.make_async_remote_copy(
+            src_ref=mine,
+            dst_ref=inbox_seq.at[rank],
+            send_sem=send_seq.at[step],
+            recv_sem=recv_seq.at[step],
+            device_id={"seq": peer},
+            device_id_type=MESH,
+        )
+
+    def start(step, carry):
+        copy(step).start()
+        return carry
+
+    def finish(step, carry):
+        copy(step).wait()
+        return carry
+
+    def start_seq(step, carry):
+        copy_seq(step).start()
+        return carry
+
+    def finish_seq(step, carry):
+        copy_seq(step).wait()
+        return carry
+
+    lax.fori_loop(1, count, start, 0)
+    lax.fori_loop(1, count, finish, 0)
+    mine[...] = jnp.sum(inbox[...], axis=0)
+    lax.fori_loop(1, group, start_seq, 0)
+    inbox_seq[pl.ds(rank, 1)] = mine[...][None]
+    lax.fori_loop(1, group, finish_seq, 0)
+    total = jnp.sum(inbox_seq[...], axis=0)
+    q_ref[...] = total[:, 0:width]
+    k_ref[...] = total[:, LANES : LANES + width]
+
+
+def reduce_gains(gains):
+    count, group = lax.axis_size("fsdp"), lax.axis_size("seq")
+    width = gains.shape[1] // count
+    q_part, k_part = pl.pallas_call(
+        lambda *refs: reduce_gains_kernel(count, group, *refs),
+        out_shape=[jax.ShapeDtypeStruct((1, width), jnp.float32)] * 2,
+        in_specs=[pl.BlockSpec(memory_space=pltpu.VMEM)],
+        out_specs=[pl.BlockSpec(memory_space=pltpu.VMEM)] * 2,
+        scratch_shapes=[
+            pltpu.VMEM((count, 1, 2 * LANES), jnp.float32),
+            pltpu.VMEM((count, 1, 2 * LANES), jnp.float32),
+            pltpu.VMEM((1, 2 * LANES), jnp.float32),
+            pltpu.VMEM((group, 1, 2 * LANES), jnp.float32),
+            pltpu.SemaphoreType.DMA((count,)),
+            pltpu.SemaphoreType.DMA((count,)),
+            pltpu.SemaphoreType.DMA((group,)),
+            pltpu.SemaphoreType.DMA((group,)),
+        ],
+        compiler_params=pltpu.CompilerParams(collective_id=1, has_side_effects=True),
+        name="reduce_gains",
+    )(gains)
+    return q_part[0], k_part[0]
 
 
 def padded(block, sides, width):
@@ -88,10 +273,8 @@
     head_size = columns // head_count
     row_count = frame_count * pixels
     factor = head_size ** (-0.5)
-    query_gain_full, key_gain_full = (
-        lax.all_gather(q_gain, "fsdp", axis=0, tiled=True),
-        lax.all_gather(k_gain, "fsdp", axis=0, tiled=True),
-    )
+    gains_full = gather_gains(q_gain, k_gain)
+    query_gain_full, key_gain_full = gains_full[0], gains_full[1]
     query_normed, query_wide, query_inv = normed(
         queries.reshape(row_count, columns), query_gain_full
     )
@@ -117,8 +300,8 @@
     value_terms = contract("hqk,qhd->khd", weights, upstream_heads)
     key_terms = contract("hqk,qhd->khd", dscores, query_heads) * factor
     partials = jnp.stack([key_terms, value_terms]).reshape(2, 3, row_count, columns)
-    from_above = shifted(partials[:, 0], "seq", -1)
-    from_below = shifted(partials[:, 2], "seq", 1)
+    from_above = shifted(partials[:, 0].astype(jnp.bfloat16), "seq", -1)
+    from_below = shifted(partials[:, 2].astype(jnp.bfloat16), "seq", 1)
     combined = partials[:, 1] + from_above + from_below
     key_grad = combined[0]
     value_grad = combined[1]
@@ -127,9 +310,7 @@
     )
     key_out, key_gain_grad = norm_back(key_grad, key_wide, key_inv, key_gain_full)
     value_out = value_grad.astype(jnp.bfloat16)
-    gain_grads = jnp.stack([query_gain_grad, key_gain_grad])
-    grouped = lax.psum(gain_grads, "seq")
-    shares = lax.psum_scatter(grouped, "fsdp", scatter_dimension=1, tiled=True)
+    shares = reduce_gains(jnp.stack([query_gain_grad, key_gain_grad]))
     out_shape = queries.shape
     return (
         query_out.reshape(out_shape),

time: 1030 us -> 191 us (0.19)
  waiting for transfers between devices: 717 us -> 33.5 us
  blocking collectives: 166 us -> 0 us
  Pallas kernels: 0 us -> 56.3 us
  starting transfers between devices: 38.1 us -> 12 us
  between operations: 15.7 us -> 1.73 us
    unnamed x2 -> x0, waiting for transfers between devices: 657 us -> none
    unnamed x1 -> x0, blocking collectives: 127 us -> none
    pallas_call x0 -> x2, Pallas kernels: none -> 56.3 us  [the longest x1 31.9 us: reduce_gains(): pl.pallas_call(lambda *refs: reduce_gains_kernel(count, group, *refs), ou...]
    psum x1 -> x0, blocking collectives: 38.4 us -> none  [local(): grouped = lax.psum(gain_grads, 'seq')]
    ppermute x2, waiting for transfers between devices: 41.3 us -> 14 us  [shifted(): lax.ppermute(value, axis, [(source, source + steps) for source in range(f...]
    ppermute x1, starting transfers between devices: 30.5 us -> 3.46 us  [padded(): lax.ppermute(lax.slice_in_dim(block, 0, width, axis=dim), axis, backward)]
  transfers between devices with their start and end apart: 5 -> 4, of which waited for: 3 -> 2; matrix products, arithmetic and copies ran while one was open for 1% -> 6% of each run, Pallas kernels for 0% -> 0%
where the time goes in v1:
time: 191 us; the launch traced here: 189 us
  Pallas kernels  56.3 us (29%)
  local copies, waits for them, and re-layouts  47.7 us (25%)
  waiting for transfers between devices  33.5 us (18%)
  other arithmetic  21.5 us (11%)
  matrix products  16.6 us (9%)
  starting transfers between devices  12 us (6%)
    pallas_call x1, Pallas kernels, reduce_gains(): pl.pallas_call(lambda *refs: reduce_gains_kernel(count, group, *refs), ou...  31.9 us
    pallas_call x1, Pallas kernels, gather_gains(): pl.pallas_call(lambda *refs: gather_gains_kernel(count, *refs), out_shape...  24.4 us
    ppermute x1, waiting for transfers between devices, padded(): lax.ppermute(lax.slice_in_dim(block, 0, width, axis=dim), axis, backward)  19.5 us
    another operation x3, local copies, waits for them, and re-layouts, local(): jnp.stack([key_terms, value_terms]).reshape(2, 3, row_count, columns)  18.6 us
    dot_general x6, matrix products, contract(): return jnp.einsum(form, left, right, preferred_element_type=jnp.float32)  16.6 us
    ppermute x2, waiting for transfers between devices, shifted(): lax.ppermute(value, axis, [(source, source + steps) for source in range(f...  14 us
    another operation x2, local copies, waits for them, and re-layouts, local(): near_values = key_window[1].reshape(wide_view)  8.66 us
    another operation x2, local copies, waits for them, and re-layouts, local(): near_keys = key_window[0].reshape(wide_view)  5.72 us
  transfers between devices with their start and end apart: 4, of which 2 were waited for; matrix products, arithmetic and copies ran while one was open for 6% of the time, Pallas kernels for 0%

profile of v1, /device:TPU:1, one launch (start us, length us, event | category | flops | bytes accessed | tf_op | source)
XLA Modules:
  0.0 189.4 jit_solution(1756617330855254718)
XLA Ops:
  0.7 1.4 fusion.11
  2.1 24.4 %gather_gains.1 = f32[2,2560]{1,0:T(2,128)} custom-call(f32[1,80]{1,0:T(1,128)} %bitcast.131, f32[1,80]{1,0:T(1,128)} %bitcast.132), custom_call_target="tpu_custom_call" | custom-call | tf_op jit(solution)/shard_map/gather_gains/pallas_call | solution.py:72
  28.8 3.5 %collective-permute-start.1 = (bf16[2,1,1,128,2560]{4,3,0,2,1:T(8,128)(2,1)S(1)}, bf16[2,1,1,128,2560]{4,3,0,2,1:T(8,128)(2,1)}, u32[]{:S(2)}, u32[]{:S(2)}) collective-permute-start(bf16[2,1,1,128,2560]{4,3,0,2,1:T(8,128)(2,1)S(1)} %maximum_bitcast_fusion), channel_id=1, source_target_pairs={{1,0},{2,1},{3,2},{4,3},{5,4},{6,5},{7,6},{8,7},{9,8},{10,9},{11,1... | collective-permute-start | bytes 3932168 | tf_op jit(solution)/shard_map/ppermute | solution.py:204
  32.3 3.0 %collective-permute-start = (bf16[2,1,1,128,2560]{4,3,0,2,1:T(8,128)(2,1)S(1)}, bf16[2,1,1,128,2560]{4,3,0,2,1:T(8,128)(2,1)}, u32[]{:S(2)}, u32[]{:S(2)}) collective-permute-start(bf16[2,1,1,128,2560]{4,3,0,2,1:T(8,128)(2,1)S(1)} %maximum_bitcast_fusion), channel_id=1, source_target_pairs={{0,1},{1,2},{2,3},{3,4},{4,5},{5,6},{6,7},{7,8},{8,9},{9,10},{10,1... | collective-permute-start | bytes 3932168 | tf_op jit(solution)/shard_map/ppermute | solution.py:201
  36.6 2.2 %copy.27 = bf16[1,1,128,2560]{2,3,1,0:T(8,128)(2,1)} copy(bf16[1,1,128,2560]{3,2,1,0:T(8,128)(2,1)} %param.11) | data formatting | bytes 1310720 | tf_op args[3]
  40.3 19.5 %collective-permute-done.1 = bf16[2,1,1,128,2560]{4,3,0,2,1:T(8,128)(2,1)} collective-permute-done((bf16[2,1,1,128,2560]{4,3,0,2,1:T(8,128)(2,1)S(1)}, bf16[2,1,1,128,2560]{4,3,0,2,1:T(8,128)(2,1)}, u32[]{:S(2)}, u32[]{:S(2)}) %collective-permute-start.1) | collective-permute-done | bytes 1310752 | tf_op jit(solution)/shard_map/ppermute | solution.py:204
  59.8 2.1 %pad_maximum_fusion.1 = bf16[2,1,3,128,2560]{4,3,0,2,1:T(8,128)(2,1)S(1)} fusion(bf16[2,1,1,128,2560]{4,3,0,2,1:T(8,128)(2,1)} %collective-permute-done.1, bf16[2,1,1,128,2560]{4,3,0,2,1:T(8,128)(2,1)S(1)} %maximum_bitcast_fusion, bf16[2,1,1,128,2560]{4,3,0,2,1:T(8,128)(2,1)} %collective-permute-done), kind=kLoop, calls=%fused_computation.4 | loop fusion | flops 3932160 | bytes 7864320 | tf_op jit(solution)/shard_map/concatenate | solution.py:205
  61.9 1.5 fusion.46
  63.4 4.3 %reshape_squeeze.7 = bf16[384,20,128]{2,1,0:T(8,128)(2,1)} reshape(bf16[1,1,3,128,2560]{4,3,0,2,1:T(8,128)(2,1)} %get-tuple-element.17) | data formatting | bytes 3932160 | tf_op jit(solution)/shard_map/reshape;squeeze | solution.py:291
  67.8 4.3 %copy.30 = bf16[384,20,128]{0,2,1:T(8,128)(2,1)} copy(bf16[384,20,128]{2,1,0:T(8,128)(2,1)} %reshape_squeeze.7) | data formatting | bytes 3932160 | tf_op jit(solution)/shard_map/reshape;squeeze | solution.py:291
  72.1 2.6 %reshape_squeeze.6 = bf16[384,20,128]{2,1,0:T(8,128)(2,1)} reshape(bf16[1,1,3,128,2560]{4,3,0,2,1:T(8,128)(2,1)S(1)} %get-tuple-element.18) | data formatting | bytes 3932160 | tf_op jit(solution)/shard_map/reshape;squeeze | solution.py:290
  74.7 3.2 %copy.32 = bf16[384,20,128]{0,2,1:T(8,128)(2,1)S(1)} copy(bf16[384,20,128]{2,1,0:T(8,128)(2,1)} %reshape_squeeze.6) | data formatting | bytes 3932160 | tf_op jit(solution)/shard_map/reshape;squeeze | solution.py:290
  77.9 3.4 %select_reduce_fusion.1 = (f32[20,128]{1,0:T(8,128)S(1)}, f32[20,128,384]{2,1,0:T(8,128)S(1)}) fusion(pred[128]{0:T(512)(128)(4,1)S(1)} %compare_and_fusion, pred[384]{0:T(512)(128)(4,1)S(1)} %compare_and_fusion.1, s32[20]{0:T(128)S(1)} %get-tuple-element.20, s32[128,384]{1,0:T(8,128)} %copy-done.7, s32[20]{0:T(128)S(1)} %get-tuple-element.21, ...), kind=kOutput, calls=%fused_computation.10 | convolution fusion | flops 262469120 | bytes 7820528 | tf_op jit(solution)/shard_map/qhd,khd->hqk/dot_general | solution.py:236
  81.3 2.4 %select_reduce_fusion = f32[20,128]{1,0:T(8,128)S(1)} fusion(f32[20,128,384]{2,1,0:T(8,128)S(1)} %get-tuple-element.23, f32[20,128]{1,0:T(8,128)S(1)} %broadcast_select_fusion, pred[128]{0:T(512)(128)(4,1)S(1)} %compare_and_fusion, pred[384]{0:T(512)(128)(4,1)S(1)} %compare_and_fusion.1, s32[20]{0:T(128)S(1)} %get-tuple-element.20, ...), kind=kLoop, calls=%fused_computation.9 | loop fusion | flops 10810880 | bytes 4543216 | tf_op jit(solution)/shard_map/reduce_sum | solution.py:244
  83.8 2.4 %convolution_bitcast_fusion = f32[384,20,128]{2,0,1:T(8,128)S(1)} fusion(bf16[128,20,128]{0,2,1:T(8,128)(2,1)S(1)} %bitcast.124, f32[20,128,384]{2,1,0:T(8,128)S(1)} %get-tuple-element.23, f32[20,128]{1,0:T(8,128)S(1)} %log_add_fusion, s32[128,384]{1,0:T(8,128)S(1)} %copy-done.8, s32[128,384]{1,0:T(8,128)S(1)} %copy-done.10, ...), kind=kOutput, calls=%fused_computation.17 | convolution fusion | flops 262471680 | bytes 9120496 | tf_op jit(solution)/shard_map/hqk,qhd->khd/dot_general | solution.py:236
  86.3 2.6 %fusion.26 = f32[128,20]{0,1:T(8,128)S(1)} fusion(bf16[384,20,128]{0,2,1:T(8,128)(2,1)S(1)} %copy-done.6, bf16[128,20,128]{0,2,1:T(8,128)(2,1)S(1)} %bitcast.125, f32[20,128,384]{2,1,0:T(8,128)S(1)} %get-tuple-element.23, f32[20,128]{1,0:T(8,128)S(1)} %log_add_fusion, s32[128,384]{1,0:T(8,128)S(1)} %copy-done.8, s32[128,384]{1,0:T(8,128)S(1)} %copy-done.10, ...), kind=kOutput, calls=%fused_computation.52 | convolution fusion | flops 263452160 | bytes 7164656 | tf_op jit(solution)/shard_map/hqk,khd->qhd/dot_general | solution.py:236
  88.8 3.0 %fusion.1 = bf16[20,128,384]{2,1,0:T(8,128)(2,1)S(1)} fusion(f32[20,128,384]{2,1,0:T(8,128)S(1)} %get-tuple-element.23, bf16[384,20,128]{0,2,1:T(8,128)(2,1)S(1)} %copy-done.6, bf16[128,20,128]{0,2,1:T(8,128)(2,1)S(1)} %bitcast.126, f32[20,128]{1,0:T(8,128)S(1)} %bitcast.135, f32[20,128]{1,0:T(8,128)S(1)} %log_add_fusion, ...), kind=kOutput, calls=%fused_computation.6 | convolution fusion | flops 264437760 | bytes 9130736 | tf_op jit(solution)/shard_map/qhd,khd->hqk/dot_general | solution.py:236
  91.9 2.7 %multiply_bitcast_fusion = f32[384,20,128]{0,2,1:T(8,128)} fusion(bf16[20,128,384]{2,1,0:T(8,128)(2,1)S(1)} %fusion.1, f32[128,20,128]{0,2,1:T(8,128)S(1)} %bitcast.120, f32[20,128]{1,0:T(8,128)S(1)} %bitcast.128, f32[128]{0:T(128)S(1)} %add_rsqrt_fusion.1), kind=kOutput, calls=%fused_computation.7 | convolution fusion | flops 253624320 | bytes 7219712 | tf_op jit(solution)/shard_map/hqk,qhd->khd/dot_general | solution.py:236
  94.5 4.4 %copy.37 = f32[384,20,128]{2,1,0:T(8,128)} copy(f32[384,20,128]{2,0,1:T(8,128)S(1)} %convolution_bitcast_fusion) | data formatting | bytes 7864320 | tf_op jit(solution)/shard_map/hqk,qhd->khd/transpose | solution.py:236
  99.0 5.0 %stack.24 = f32[1,3,128,2560]{3,2,1,0:T(8,128)} reshape(f32[384,20,128]{2,1,0:T(8,128)} %copy.37) | data formatting | bytes 7864320 | tf_op jit(solution)/shard_map/stack | solution.py:302
  104.0 7.0 %reshape.587 = f32[1,3,128,2560]{2,1,3,0:T(4,128)} reshape(f32[384,20,128]{0,2,1:T(8,128)} %multiply_bitcast_fusion) | data formatting | bytes 7864320 | tf_op jit(solution)/shard_map/stack | solution.py:302
  111.0 6.6 %copy.45 = f32[1,3,128,2560]{3,2,1,0:T(8,128)} copy(f32[1,3,128,2560]{2,1,3,0:T(4,128)} %reshape.587) | data formatting | bytes 7864320 | tf_op jit(solution)/shard_map/stack | solution.py:302
  117.6 4.0 %fusion = bf16[2,3,128,2560]{3,2,1,0:T(8,128)(2,1)S(1)} fusion(f32[1,3,128,2560]{3,2,1,0:T(8,128)} %stack.24, f32[1,3,128,2560]{3,2,1,0:T(8,128)} %copy.45), kind=kLoop, calls=%fused_computation.3 | loop fusion | flops 1966080 | bytes 11796480 | tf_op jit(solution)/shard_map/convert.5
  121.6 1.7 slice_bitcast_fusion.1
  123.3 1.9 %collective-permute-start.2 = (bf16[2,128,2560]{2,1,0:T(8,128)(2,1)}, bf16[2,128,2560]{2,1,0:T(8,128)(2,1)}, u32[]{:S(2)}, u32[]{:S(2)}) collective-permute-start(bf16[2,128,2560]{2,1,0:T(8,128)(2,1)} %get-tuple-element.15), channel_id=1, source_target_pairs={{1,0},{2,1},{3,2},{4,3},{5,4},{6,5},{7,6},{8,7},{9,8},{10,9},{11,1... | collective-permute-start | bytes 3932168 | tf_op jit(solution)/shard_map/ppermute | solution.py:212
  125.2 3.6 %collective-permute-start.3 = (bf16[2,128,2560]{2,1,0:T(8,128)(2,1)}, bf16[2,128,2560]{2,1,0:T(8,128)(2,1)}, u32[]{:S(2)}, u32[]{:S(2)}) collective-permute-start(bf16[2,128,2560]{2,1,0:T(8,128)(2,1)} %get-tuple-element.16), channel_id=1, source_target_pairs={{0,1},{1,2},{2,3},{3,4},{4,5},{5,6},{6,7},{7,8},{8,9},{9,10},{10,1... | collective-permute-start | bytes 3932168 | tf_op jit(solution)/shard_map/ppermute | solution.py:212
  128.8 2.5 %broadcast_multiply_fusion = (f32[20,128,128]{2,1,0:T(8,128)}, f32[20,128,128]{2,1,0:T(8,128)}) fusion(bf16[384,20,128]{0,2,1:T(8,128)(2,1)S(1)} %copy.32, bf16[20,128,384]{2,1,0:T(8,128)(2,1)S(1)} %copy-done.3), kind=kOutput, calls=%fused_computation.54 | convolution fusion | flops 251985920 | bytes 6553600 | tf_op jit(solution)/shard_map/hqk,khd->qhd/dot_general | solution.py:236
  131.3 1.8 copy.33
  133.1 2.2 %fusion.25 = (f32[20,128]{1,0:T(8,128)S(1)}, f32[128]{0:T(128)S(1)}) fusion(f32[128,20,128]{0,2,1:T(8,128)S(1)} %bitcast.121, f32[128]{0:T(128)S(1)} %add_rsqrt_fusion.1, f32[20,128,128]{2,1,0:T(8,128)} %get-tuple-element.25, f32[20,128]{1,0:T(8,128)S(1)} %broadcast_multiply_fusion.1), kind=kLoop, calls=%fused_computation.48 | loop fusion | flops 2291072 | bytes 2642944 | tf_op jit(solution)/shard_map/reduce_sum | solution.py:267
  136.6 14.0 %collective-permute-done.2 = bf16[2,128,2560]{2,1,0:T(8,128)(2,1)} collective-permute-done((bf16[2,128,2560]{2,1,0:T(8,128)(2,1)}, bf16[2,128,2560]{2,1,0:T(8,128)(2,1)}, u32[]{:S(2)}, u32[]{:S(2)}) %collective-permute-start.2) | collective-permute-done | bytes 1310752 | tf_op jit(solution)/shard_map/ppermute | solution.py:212
  150.7 2.6 %fusion.5 = f32[2,128,2560]{2,1,0:T(8,128)S(1)} fusion(f32[1,3,128,2560]{3,2,1,0:T(8,128)} %copy.45, f32[1,3,128,2560]{3,2,1,0:T(8,128)S(1)} %copy-done, bf16[2,128,2560]{2,1,0:T(8,128)(2,1)} %collective-permute-done.3, bf16[2,128,2560]{2,1,0:T(8,128)(2,1)} %collective-permute-done.2), kind=kLoop, calls=%fused_computation.15 | loop fusion | flops 3276800 | bytes 13107200 | tf_op jit(solution)/shard_map/add | solution.py:305
  155.2 31.9 %reduce_gains.1 = (f32[1,80]{1,0:T(1,128)}, f32[1,80]{1,0:T(1,128)}) custom-call(f32[2,2560]{1,0:T(2,128)} %pad_maximum_fusion.2.refs_0_), custom_call_target="tpu_custom_call" | custom-call | tf_op jit(solution)/shard_map/reduce_gains/pallas_call | solution.py:175
  (67 shorter events, 9.9 us)
Async XLA Ops:
  0.6 28.1 %copy-start.11 = (bf16[1,1,128,2560]{3,2,1,0:T(8,128)(2,1)S(1)}, bf16[1,1,128,2560]{3,2,1,0:T(8,128)(2,1)}, u32[]{:S(2)}) copy-start(bf16[1,1,128,2560]{3,2,1,0:T(8,128)(2,1)} %param.10) | copy-start | bytes 1966084
  0.6 34.7 %copy-start.4 = (bf16[1,1,128,2560]{3,2,1,0:T(8,128)(2,1)S(1)}, bf16[1,1,128,2560]{3,2,1,0:T(8,128)(2,1)}, u32[]{:S(2)}) copy-start(bf16[1,1,128,2560]{3,2,1,0:T(8,128)(2,1)} %param.8) | copy-start | bytes 1966084
  28.8 9.9 %copy-start.13 = (s32[20,3]{0,1:T(4,128)S(1)}, s32[20,3]{0,1:T(4,128)}, u32[]{:S(2)}) copy-start(s32[20,3]{0,1:T(4,128)} %param.15) | copy-start | bytes 724
  28.8 31.0 %collective-permute-start.1 = (bf16[2,1,1,128,2560]{4,3,0,2,1:T(8,128)(2,1)S(1)}, bf16[2,1,1,128,2560]{4,3,0,2,1:T(8,128)(2,1)}, u32[]{:S(2)}, u32[]{:S(2)}) collective-permute-start(bf16[2,1,1,128,2560]{4,3,0,2,1:T(8,128)(2,1)S(1)} %maximum_bitcast_fusion), channel_id=1, source_target_pairs={{1,0},{2,1},{3,2},{4,3},{5,4},{6,5},{7,6},{8,7},{9,8},{10,9},{11,1... | collective-permute-start | bytes 3932168 | tf_op jit(solution)/shard_map/ppermute | solution.py:204
  32.3 27.5 %collective-permute-start = (bf16[2,1,1,128,2560]{4,3,0,2,1:T(8,128)(2,1)S(1)}, bf16[2,1,1,128,2560]{4,3,0,2,1:T(8,128)(2,1)}, u32[]{:S(2)}, u32[]{:S(2)}) collective-permute-start(bf16[2,1,1,128,2560]{4,3,0,2,1:T(8,128)(2,1)S(1)} %maximum_bitcast_fusion), channel_id=1, source_target_pairs={{0,1},{1,2},{2,3},{3,4},{4,5},{5,6},{6,7},{7,8},{8,9},{9,10},{10,1... | collective-permute-start | bytes 3932168 | tf_op jit(solution)/shard_map/ppermute | solution.py:201
  39.0 20.8 %copy-start.7 = (s32[128,384]{1,0:T(8,128)}, s32[128,384]{1,0:T(8,128)S(1)}, u32[]{:S(2)}) copy-start(s32[128,384]{1,0:T(8,128)S(1)} %get-tuple-element.26) | copy-start | bytes 589828
  39.0 20.8 %copy-start.9 = (s32[128,384]{1,0:T(8,128)}, s32[128,384]{1,0:T(8,128)S(1)}, u32[]{:S(2)}) copy-start(s32[128,384]{1,0:T(8,128)S(1)} %get-tuple-element.27) | copy-start | bytes 589828
  77.8 3.5 %copy-start.8 = (s32[128,384]{1,0:T(8,128)S(1)}, s32[128,384]{1,0:T(8,128)}, u32[]{:S(2)}) copy-start(s32[128,384]{1,0:T(8,128)} %copy-done.7) | copy-start | bytes 589828
  77.8 3.5 %copy-start.10 = (s32[128,384]{1,0:T(8,128)S(1)}, s32[128,384]{1,0:T(8,128)}, u32[]{:S(2)}) copy-start(s32[128,384]{1,0:T(8,128)} %copy-done.9) | copy-start | bytes 589828
  81.3 2.5 %copy-start.12 = (bf16[1,1,128,2560]{2,3,1,0:T(8,128)(2,1)S(1)}, bf16[1,1,128,2560]{2,3,1,0:T(8,128)(2,1)}, u32[]{:S(2)}) copy-start(bf16[1,1,128,2560]{2,3,1,0:T(8,128)(2,1)} %copy.27) | copy-start | bytes 1966084
  83.8 2.5 %copy-start.6 = (bf16[384,20,128]{0,2,1:T(8,128)(2,1)S(1)}, bf16[384,20,128]{0,2,1:T(8,128)(2,1)}, u32[]{:S(2)}) copy-start(bf16[384,20,128]{0,2,1:T(8,128)(2,1)} %copy.30) | copy-start | bytes 5898244
  91.9 2.7 %copy-start.2 = (bf16[20,128,384]{2,1,0:T(8,128)(2,1)}, bf16[20,128,384]{2,1,0:T(8,128)(2,1)S(1)}, u32[]{:S(2)}) copy-start(bf16[20,128,384]{2,1,0:T(8,128)(2,1)S(1)} %fusion.1) | copy-start | bytes 5898244
  121.6 7.3 %copy-start.3 = (bf16[20,128,384]{2,1,0:T(8,128)(2,1)S(1)}, bf16[20,128,384]{2,1,0:T(8,128)(2,1)}, u32[]{:S(2)}) copy-start(bf16[20,128,384]{2,1,0:T(8,128)(2,1)} %copy-done.2) | copy-start | bytes 5898244
  123.3 27.4 %collective-permute-start.2 = (bf16[2,128,2560]{2,1,0:T(8,128)(2,1)}, bf16[2,128,2560]{2,1,0:T(8,128)(2,1)}, u32[]{:S(2)}, u32[]{:S(2)}) collective-permute-start(bf16[2,128,2560]{2,1,0:T(8,128)(2,1)} %get-tuple-element.15), channel_id=1, source_target_pairs={{1,0},{2,1},{3,2},{4,3},{5,4},{6,5},{7,6},{8,7},{9,8},{10,9},{11,1... | collective-permute-start | bytes 3932168 | tf_op jit(solution)/shard_map/ppermute | solution.py:212
  125.2 25.5 %collective-permute-start.3 = (bf16[2,128,2560]{2,1,0:T(8,128)(2,1)}, bf16[2,128,2560]{2,1,0:T(8,128)(2,1)}, u32[]{:S(2)}, u32[]{:S(2)}) collective-permute-start(bf16[2,128,2560]{2,1,0:T(8,128)(2,1)} %get-tuple-element.16), channel_id=1, source_target_pairs={{0,1},{1,2},{2,3},{3,4},{4,5},{5,6},{6,7},{7,8},{8,9},{9,10},{10,1... | collective-permute-start | bytes 3932168 | tf_op jit(solution)/shard_map/ppermute | solution.py:212
  131.3 4.1 %copy-start.5 = (bf16[1,1,128,2560]{3,2,1,0:T(8,128)(2,1)S(1)}, bf16[1,1,128,2560]{3,2,1,0:T(8,128)(2,1)}, u32[]{:S(2)}) copy-start(bf16[1,1,128,2560]{3,2,1,0:T(8,128)(2,1)} %param.8) | copy-start | bytes 1966084
  133.1 17.6 %copy-start = (f32[1,3,128,2560]{3,2,1,0:T(8,128)S(1)}, f32[1,3,128,2560]{3,2,1,0:T(8,128)}, u32[]{:S(2)}) copy-start(f32[1,3,128,2560]{3,2,1,0:T(8,128)} %stack.24) | copy-start | bytes 11796484
  136.6 16.6 %copy-start.1 = (bf16[1,1,128,2560]{3,2,1,0:T(8,128)(2,1)S(1)}, bf16[1,1,128,2560]{3,2,1,0:T(8,128)(2,1)}, u32[]{:S(2)}) copy-start(bf16[1,1,128,2560]{3,2,1,0:T(8,128)(2,1)} %param.9) | copy-start | bytes 1966084
  187.1 1.2 copy-start.15
  187.2 1.7 copy-start.14

commit v2 on v0

v2 whole, which is shorter than its diff:
```python
import functools

import jax
import jax.numpy as jnp
from jax import lax
from jax.experimental import pallas as pl
from jax.experimental.pallas import tpu as pltpu
from jax.sharding import PartitionSpec as P

PW = 8
TILE_H = 4
TILE_W = 4
LANES = 128
EPS = 1e-06
BLOCKED = -1e30
FLOOR = -1e29
MESH = pl.DeviceIdType.MESH
KEYS, VALUES, QUERIES, UPSTREAM = range(4)


def dot(left, right, left_dim, right_dim):
    return lax.dot_general(
        left, right, (((left_dim,), (right_dim,)), ((), ())), preferred_element_type=jnp.float32
    )


def attention_kernel(
    far,
    count,
    group,
    limits,
    queries,
    keys,
    values,
    upstream,
    q_gain,
    k_gain,
    d_queries,
    d_keys,
    d_values,
    d_q_gain,
    d_k_gain,
    key_raw,
    query_raw,
    key_own,
    query_own,
    value_own,
    upstream_own,
    key_in,
    value_in,
    query_in,
    upstream_in,
    stat_out,
    stat_in,
    inverse_out,
    inverse_in,
    inverse_own,
    inverse_near,
    gains,
    gain_rows,
    query_grad,
    key_grad,
    value_grad,
    gain_mine,
    gain_inbox,
    sum_outbox,
    sum_inbox,
    sum_mine,
    sum_inbox_seq,
    send_sem,
    recv_sem,
    stat_send,
    stat_recv,
    inverse_send,
    inverse_recv,
    gain_send,
    gain_recv,
    sum_send,
    sum_recv,
    seq_send,
    seq_recv,
):
    me = lax.axis_index("fsdp")
    rank = lax.axis_index("seq")
    heads = limits.shape[0]
    rows, columns = queries.shape
    size = columns // heads
    width = q_gain.shape[1]
    factor = size ** (-0.5)
    far_pairs, pairs = far // 2, heads // 2
    below, above = lax.rem(rank + group - 1, group), lax.rem(rank + 1, group)
    barrier = pltpu.get_barrier_semaphore()

    def repeat(first, last, body):
        lax.fori_loop(first, last, lambda step, carry: (body(step), carry)[1], 0)

    def of_head(ref, head):
        return ref[:, pl.ds(pl.multiple_of(head * size, size), size)]

    outgoing = (key_raw, value_own, query_raw, upstream_own)
    incoming = (key_in, value_in, query_in, upstream_in)

    def link(which, side, pair):
        part = pl.ds(2 * pair, 2)
        return pltpu.make_async_remote_copy(
            src_ref=outgoing[which].at[part],
            dst_ref=incoming[which].at[1 - side, part],
            send_sem=send_sem.at[which, side, pair],
            recv_sem=recv_sem.at[which, 1 - side, pair],
            device_id={"seq": above if side else below},
            device_id_type=MESH,
        )

    def stat_link(side, pair):
        part = pl.ds(2 * pair, 2)
        return pltpu.make_async_remote_copy(
            src_ref=stat_out.at[part],
            dst_ref=stat_in.at[1 - side, part],
            send_sem=stat_send.at[side, pair],
            recv_sem=stat_recv.at[1 - side, pair],
            device_id={"seq": above if side else below},
            device_id_type=MESH,
        )

    def inverse_link(side):
        return pltpu.make_async_remote_copy(
            src_ref=inverse_out,
            dst_ref=inverse_in.at[1 - side],
            send_sem=inverse_send.at[side],
            recv_sem=inverse_recv.at[1 - side],
            device_id={"seq": above if side else below},
            device_id_type=MESH,
        )

    def gain_link(step):
        return pltpu.make_async_remote_copy(
            src_ref=gain_mine,
            dst_ref=gain_inbox.at[me],
            send_sem=gain_send.at[step],
            recv_sem=gain_recv.at[step],
            device_id={"fsdp": lax.rem(me + step, count)},
            device_id_type=MESH,
        )

    def sum_link(step):
        peer = lax.rem(me + step, count)
        return pltpu.make_async_remote_copy(
            src_ref=sum_outbox.at[peer],
            dst_ref=sum_inbox.at[me],
            send_sem=sum_send.at[step],
            recv_sem=sum_recv.at[step],
            device_id={"fsdp": peer},
            device_id_type=MESH,
        )

    def seq_link(step):
        return pltpu.make_async_remote_copy(
            src_ref=sum_mine,
            dst_ref=sum_inbox_seq.at[rank],
            send_sem=seq_send.at[step],
            recv_sem=seq_recv.at[step],
            device_id={"seq": lax.rem(rank + step, group)},
            device_id_type=MESH,
        )

    def greet(step):
        peer = lax.rem(me + step, count)
        pl.semaphore_signal(barrier, inc=1, device_id={"fsdp": peer}, device_id_type=MESH)

    def greet_seq(step):
        peer = lax.rem(rank + step, group)
        pl.semaphore_signal(barrier, inc=1, device_id={"seq": peer}, device_id_type=MESH)

    repeat(1, count, greet)
    repeat(1, group, greet_seq)

    def stage_keys(slot):
        key_raw[slot] = of_head(keys, slot)
        value_own[slot] = of_head(values, slot)

    def stage_queries(slot):
        query_raw[slot] = of_head(queries, slot)
        upstream_own[slot] = of_head(upstream, slot)

    repeat(0, heads, stage_keys)
    gain_mine[...] = jnp.zeros_like(gain_mine)
    gain_mine[0:1, 0:width] = q_gain[...]
    gain_mine[0:1, LANES : LANES + width] = k_gain[...]
    gain_inbox[pl.ds(me, 1)] = gain_mine[...][None]
    pl.semaphore_wait(barrier, count + group - 2)

    def send_keys(pair):
        for side in range(2):
            link(KEYS, side, pair).start()
            link(VALUES, side, pair).start()

    def send_queries(pair):
        for side in range(2):
            link(QUERIES, side, pair).start()
            link(UPSTREAM, side, pair).start()

    repeat(1, count, lambda step: gain_link(step).start())
    repeat(0, far_pairs, send_keys)
    repeat(0, heads, stage_queries)

    for row, ref in enumerate((queries, keys)):

        def squares(head, total):
            wide = of_head(ref, head).astype(jnp.float32)
            return total + wide * wide

        total = lax.fori_loop(0, heads, squares, jnp.zeros((rows, size), jnp.float32))
        mean = jnp.sum(total, axis=1, keepdims=True) / columns
        inverse = jnp.broadcast_to(lax.rsqrt(mean + EPS), (rows, size))
        inverse_own[row] = inverse
        inverse_out[row : row + 1, :] = jnp.transpose(inverse)[0:1, :]
    for side in range(2):
        inverse_link(side).start()

    repeat(1, count, lambda step: gain_link(step).wait())
    lane = lax.broadcasted_iota(jnp.int32, (1, LANES), 1)
    for row in range(2):
        tiles = [jnp.zeros((1, LANES), jnp.float32) for _ in range(heads + 1)]
        for owner in range(count):
            tile, offset = divmod(owner * width, LANES)
            part = gain_inbox[owner, :, row * LANES : (row + 1) * LANES]
            if offset:
                part = pltpu.roll(part, offset, 1)
            if offset + width > LANES:
                tiles[tile + 1] = tiles[tile + 1] + jnp.where(lane < offset, part, 0.0)
                part = jnp.where(lane >= offset, part, 0.0)
            tiles[tile] = tiles[tile] + part
        for head in range(heads):
            gains[row, head] = tiles[head]

    def normed(raw, inverse, row, head):
        return (raw.astype(jnp.float32) * inverse * gains[row, head]).astype(jnp.bfloat16)

    def normalise(slot):
        query_own[slot] = normed(query_raw[slot], inverse_own[0], 0, slot)
        key_own[slot] = normed(key_raw[slot], inverse_own[1], 1, slot)

    repeat(0, heads, normalise)

    key_pixel = lax.broadcasted_iota(jnp.int32, (rows, rows), 0)
    query_pixel = lax.broadcasted_iota(jnp.int32, (rows, rows), 1)
    apart_rows = jnp.abs(key_pixel // PW // TILE_H - query_pixel // PW // TILE_H)
    apart_columns = jnp.abs(key_pixel % PW // TILE_W - query_pixel % PW // TILE_W)
    apart_rows = apart_rows.astype(jnp.float32)
    apart_columns = apart_columns.astype(jnp.float32)

    def spatial(head):
        seen = (apart_rows <= limits[head, 3:4, :]) & (apart_columns <= limits[head, 4:5, :])
        return jnp.where(seen, 0.0, BLOCKED)

    def frame_bias(head, frame):
        return limits[head, frame : frame + 1, :]

    def soft(scores, bias):
        scores = scores * factor + bias
        top = jnp.maximum(jnp.max(scores, axis=0, keepdims=True), FLOOR)
        raised = jnp.exp(scores - top)
        total = jnp.maximum(jnp.sum(raised, axis=0, keepdims=True), 1e-30)
        return raised * (1.0 / total), top + jnp.log(total)

    def query_side(slot, key_all, value_all, bias, own):
        query_block, upstream_block = query_own[slot], upstream_own[slot]
        probs, logsum = soft(dot(key_all, query_block, 1, 1), bias)
        weights = probs.astype(jnp.bfloat16)
        dprobs = dot(value_all, upstream_block, 1, 1)
        deltas = jnp.sum(weights.astype(jnp.float32) * dprobs, axis=0, keepdims=True)
        dscores = (probs * (dprobs - deltas)).astype(jnp.bfloat16)
        query_grad[slot] = dot(dscores, key_all, 0, 0) * factor
        key_grad[slot] = dot(dscores[own], query_block, 1, 0) * factor
        value_grad[slot] = dot(weights[own], upstream_block, 1, 0)
        return logsum, deltas

    def alone(pair):
        for slot in (2 * pair, 2 * pair + 1):
            bias = spatial(slot) + frame_bias(slot, 1)
            query_side(slot, key_own[slot], value_own[slot], bias, slice(0, rows))

    if far_pairs < pairs:
        repeat(far_pairs, pairs, alone)

    for side in range(2):
        inverse_link(1 - side).wait_recv()
        for row in range(2):
            spread = jnp.broadcast_to(inverse_in[side, row : row + 1, :], (rows, size))
            inverse_near[side, row] = jnp.transpose(spread)

    def near_queries(pair):
        for side in range(2):
            link(KEYS, 1 - side, pair).wait_recv()
            link(VALUES, 1 - side, pair).wait_recv()
        send_queries(pair)
        for slot in (2 * pair, 2 * pair + 1):
            low = normed(key_in[0, slot], inverse_near[0, 1], 1, slot)
            high = normed(key_in[1, slot], inverse_near[1, 1], 1, slot)
            key_all = jnp.concatenate([low, key_own[slot], high], axis=0)
            value_all = jnp.concatenate([value_in[0, slot], value_own[slot], value_in[1, slot]], axis=0)
            bias = spatial(slot)
            bias = jnp.concatenate([bias + frame_bias(slot, at) for at in range(3)], axis=0)
            logsum, deltas = query_side(slot, key_all, value_all, bias, slice(rows, 2 * rows))
            stat_out[slot, 0:1, :] = logsum
            stat_out[slot, 1:2, :] = deltas
        for side in range(2):
            stat_link(side, pair).start()

    repeat(0, far_pairs, near_queries)

    def norm_back(row, ref, grad, out):
        inverse = inverse_own[row]

        def first(head, total):
            wide, slope = of_head(ref, head).astype(jnp.float32), grad[head]
            gain_rows[row, head] = jnp.sum(slope * wide * inverse, axis=0, keepdims=True)
            return total + slope * gains[row, head] * wide

        total = lax.fori_loop(0, heads, first, jnp.zeros((rows, size), jnp.float32))
        inner = jnp.sum(total, axis=1, keepdims=True) / columns
        shrink = inverse * inverse * inner

        def second(head):
            wide, slope = of_head(ref, head).astype(jnp.float32), grad[head]
            result = inverse * (slope * gains[row, head] - wide * shrink)
            out[:, pl.ds(pl.multiple_of(head * size, size), size)] = result.astype(jnp.bfloat16)

        repeat(0, heads, second)

    norm_back(0, queries, query_grad, d_queries)

    def near_keys(pair):
        for side in range(2):
            link(QUERIES, 1 - side, pair).wait_recv()
            link(UPSTREAM, 1 - side, pair).wait_recv()
            stat_link(1 - side, pair).wait_recv()
        for slot in (2 * pair, 2 * pair + 1):
            low = normed(query_in[0, slot], inverse_near[0, 0], 0, slot)
            high = normed(query_in[1, slot], inverse_near[1, 0], 0, slot)
            query_all = jnp.concatenate([low, high], axis=0)
            upstream_all = jnp.concatenate([upstream_in[0, slot], upstream_in[1, slot]], axis=0)
            bias = spatial(slot)
            bias = jnp.concatenate(
                [
                    bias + (frame_bias(slot, 0) - stat_in[0, slot, 0:1, :]),
                    bias + (frame_bias(slot, 2) - stat_in[1, slot, 0:1, :]),
                ],
                axis=1,
            )
            deltas = jnp.concatenate([stat_in[0, slot, 1:2, :], stat_in[1, slot, 1:2, :]], axis=1)
            probs = jnp.exp(dot(key_own[slot], query_all, 1, 1) * factor + bias)
            weights = probs.astype(jnp.bfloat16)
            dprobs = dot(value_own[slot], upstream_all, 1, 1)
            dscores = (probs * (dprobs - deltas)).astype(jnp.bfloat16)
            key_grad[slot] += dot(dscores, query_all, 1, 0) * factor
            value_grad[slot] += dot(weights, upstream_all, 1, 0)

    repeat(0, far_pairs, near_keys)
    norm_back(1, keys, key_grad, d_keys)

    for owner in range(count):
        tile, offset = divmod(owner * width, LANES)
        for row in range(2):
            part = gain_rows[row, tile]
            if offset:
                part = pltpu.roll(part, LANES - offset, 1)
            if offset + width > LANES:
                after = pltpu.roll(gain_rows[row, tile + 1], LANES - offset, 1)
                part = jnp.where(lane < LANES - offset, part, after)
            sum_outbox[owner, :, row * LANES : (row + 1) * LANES] = part
    sum_inbox[pl.ds(me, 1)] = sum_outbox[pl.ds(me, 1)]
    repeat(1, count, lambda step: sum_link(step).start())

    def finish_values(head):
        out = value_grad[head].astype(jnp.bfloat16)
        d_values[:, pl.ds(pl.multiple_of(head * size, size), size)] = out

    repeat(0, heads, finish_values)
    repeat(1, count, lambda step: sum_link(step).wait())
    sum_mine[...] = jnp.sum(sum_inbox[...], axis=0)
    repeat(1, group, lambda step: seq_link(step).start())
    sum_inbox_seq[pl.ds(rank, 1)] = sum_mine[...][None]

    def sent(pair):
        for side in range(2):
            for which in range(4):
                link(which, side, pair).wait_send()
            stat_link(side, pair).wait_send()

    repeat(0, far_pairs, sent)
    for side in range(2):
        inverse_link(side).wait_send()
    repeat(1, group, lambda step: seq_link(step).wait())
    total = jnp.sum(sum_inbox_seq[...], axis=0)
    d_q_gain[...] = total[:, 0:width]
    d_k_gain[...] = total[:, LANES : LANES + width]


def attention(far, identity, limits, queries, keys, values, upstream, q_gain, k_gain):
    count, group = lax.axis_size("fsdp"), lax.axis_size("seq")
    heads = limits.shape[0]
    rows, columns = queries.shape
    size = columns // heads
    width = q_gain.shape[0]
    wide, narrow = jnp.float32, jnp.bfloat16
    pairs = max(far // 2, 1)
    vmem = pl.BlockSpec(memory_space=pltpu.VMEM)
    block = (rows, size)
    dma = pltpu.SemaphoreType.DMA
    scratch = [
        pltpu.VMEM((heads,) + block, narrow),
        pltpu.VMEM((heads,) + block, narrow),
        pltpu.VMEM((heads,) + block, narrow),
        pltpu.VMEM((heads,) + block, narrow),
        pltpu.VMEM((heads,) + block, narrow),
        pltpu.VMEM((heads,) + block, narrow),
        pltpu.VMEM((2, far) + block, narrow),
        pltpu.VMEM((2, far) + block, narrow),
        pltpu.VMEM((2, far) + block, narrow),
        pltpu.VMEM((2, far) + block, narrow),
        pltpu.VMEM((far, 2, size), wide),
        pltpu.VMEM((2, far, 2, size), wide),
        pltpu.VMEM((2, size), wide),
        pltpu.VMEM((2, 2, size), wide),
        pltpu.VMEM((2,) + block, wide),
        pltpu.VMEM((2, 2) + block, wide),
        pltpu.VMEM((2, heads, 1, size), wide),
        pltpu.VMEM((2, heads, 1, size), wide),
        pltpu.VMEM((heads,) + block, wide),
        pltpu.VMEM((heads,) + block, wide),
        pltpu.VMEM((heads,) + block, wide),
        pltpu.VMEM((1, 2 * LANES), wide),
        pltpu.VMEM((count, 1, 2 * LANES), wide),
        pltpu.VMEM((count, 1, 2 * LANES), wide),
        pltpu.VMEM((count, 1, 2 * LANES), wide),
        pltpu.VMEM((1, 2 * LANES), wide),
        pltpu.VMEM((group, 1, 2 * LANES), wide),
        dma((4, 2, pairs)),
        dma((4, 2, pairs)),
        dma((2, pairs)),
        dma((2, pairs)),
        dma((2,)),
        dma((2,)),
        dma((count,)),
        dma((count,)),
        dma((count,)),
        dma((count,)),
        dma((group,)),
        dma((group,)),
    ]
    d_queries, d_keys, d_values, d_q_gain, d_k_gain = pl.pallas_call(
        functools.partial(attention_kernel, far, count, group),
        out_shape=[jax.ShapeDtypeStruct((rows, columns), narrow)] * 3
        + [jax.ShapeDtypeStruct((1, width), wide)] * 2,
        in_specs=[vmem] * 7,
        out_specs=[vmem] * 5,
        scratch_shapes=scratch,
        compiler_params=pltpu.CompilerParams(
            collective_id=identity, has_side_effects=True, vmem_limit_bytes=48 * 1024 * 1024
        ),
        name="attention_backward",
    )(limits, queries, keys, values, upstream, q_gain[None], k_gain[None])
    return d_queries, d_keys, d_values, d_q_gain[0], d_k_gain[0]


def head_limits(windows, frames):
    rank, group = lax.axis_index("seq"), lax.axis_size("seq")
    near = windows[:, 0] >= 1
    own = jnp.full_like(near, rank < frames)
    below = near & (rank > 0) & (rank < frames)
    above = near & (rank + 1 < group) & (rank + 1 < frames)
    blocks = jnp.where(jnp.stack([below, own, above], 1), 0.0, BLOCKED)
    table = jnp.concatenate([blocks, windows.astype(jnp.float32)[:, 1:], jnp.zeros_like(blocks)], 1)
    return jnp.broadcast_to(table[:, :, None], table.shape + (LANES,))


def local(queries, keys, values, grad_out, q_gain, k_gain, lengths, windows):
    shape = queries.shape
    flat = (shape[1] * shape[2], shape[3])
    arrays = [array.reshape(flat) for array in (queries, keys, values, grad_out)]
    limits = head_limits(windows, lengths[0])
    heads = windows.shape[0]
    d_queries, d_keys, d_values, d_q_gain, d_k_gain = attention(
        heads, 0, limits, *arrays, q_gain, k_gain
    )
    return (
        d_queries.reshape(shape),
        d_keys.reshape(shape),
        d_values.reshape(shape),
        d_q_gain,
        d_k_gain,
    )


def solution(mesh):
    in_specs = (
        P("fsdp", "seq", None, None),
        P("fsdp", "seq", None, None),
        P("fsdp", "seq", None, None),
        P("fsdp", "seq", None, None),
        P("fsdp"),
        P("fsdp"),
        P("fsdp"),
        P(),
    )
    out_specs = (
        P("fsdp", "seq", None, None),
        P("fsdp", "seq", None, None),
        P("fsdp", "seq", None, None),
        P("fsdp"),
        P("fsdp"),
    )
    return jax.shard_map(local, mesh=mesh, in_specs=in_specs, out_specs=out_specs, check_vma=False)
```

time: 1030 us -> 106 us (0.10)
  waiting for transfers between devices: 717 us -> 0 us
  blocking collectives: 166 us -> 0 us
  Pallas kernels: 0 us -> 95.2 us
  local copies, waits for them, and re-layouts: 50 us -> 9.31 us
  starting transfers between devices: 38.1 us -> 0 us
  other arithmetic: 24.2 us -> 0.04 us
  matrix products: 16.6 us -> 0 us
  between operations: 15.7 us -> 1.35 us
    unnamed x2 -> x0, waiting for transfers between devices: 657 us -> none
    unnamed x1 -> x0, blocking collectives: 127 us -> none
    pallas_call x0 -> x1, Pallas kernels: none -> 95.2 us  [attention(): pl.pallas_call(functools.partial(attention_kernel, far, count, group), ou...]
    ppermute x4 -> x0, waiting for transfers between devices: 59.9 us -> none  [the longest x2 41.3 us: shifted(): lax.ppermute(value, axis, [(source, source + steps) for source in range(f...]
    psum x1 -> x0, blocking collectives: 38.4 us -> none  [local(): grouped = lax.psum(gain_grads, 'seq')]
    ppermute x4 -> x0, starting transfers between devices: 38.1 us -> none  [the longest x1 30.5 us: padded(): lax.ppermute(lax.slice_in_dim(block, 0, width, axis=dim), axis, backward)]
    another operation x8 -> x0, local copies, waits for them, and re-layouts: 33 us -> none  [the longest x3 18.6 us: local(): jnp.stack([key_terms, value_terms]).reshape(2, 3, row_count, columns)]
    dot_general x6 -> x0, matrix products: 16.6 us -> none  [contract(): return jnp.einsum(form, left, right, preferred_element_type=jnp.float32)]
  transfers between devices with their start and end apart: 5 -> 0, of which waited for: 3 -> 0; matrix products, arithmetic and copies ran while one was open for 1% -> 0% of each run, Pallas kernels for 0% -> 0%
where the time goes in v2:
time: 106 us
  Pallas kernels  95.2 us (90%)
  local copies, waits for them, and re-layouts  9.31 us (9%)
  between operations  1.35 us (1%)
    pallas_call x1, Pallas kernels, attention(): pl.pallas_call(functools.partial(attention_kernel, far, count, group), ou...  95.2 us
    unnamed x19, local copies, waits for them, and re-layouts  9.14 us

profile of v2, /device:TPU:1, one launch (start us, length us, event | category | flops | bytes accessed | tf_op | source)
XLA Modules:
  0.0 105.9 jit_solution(7560333782754852385)
XLA Ops:
  1.3 0.0 copy-start.6
  1.3 0.7 copy-done.6
  2.0 0.1 copy.13
  2.1 0.0 copy-start.4
  2.1 0.0 copy-start.5
  2.1 0.1 broadcast_in_dim.23.limits
  2.2 0.6 copy-done.4
  2.8 0.0 copy-done.5
  2.8 0.0 copy-start
  2.8 1.1 %copy-done = bf16[1,1,128,2560]{3,2,1,0:T(8,128)(2,1)S(1)} copy-done((bf16[1,1,128,2560]{3,2,1,0:T(8,128)(2,1)S(1)}, bf16[1,1,128,2560]{3,2,1,0:T(8,128)(2,1)}, u32[]{:S(2)}) %copy-start) | copy-done | bytes 655384
  3.9 0.0 copy-start.1
  3.9 1.1 %copy-done.1 = bf16[1,1,128,2560]{3,2,1,0:T(8,128)(2,1)S(1)} copy-done((bf16[1,1,128,2560]{3,2,1,0:T(8,128)(2,1)S(1)}, bf16[1,1,128,2560]{3,2,1,0:T(8,128)(2,1)}, u32[]{:S(2)}) %copy-start.1) | copy-done | bytes 655384
  5.0 0.0 copy-start.2
  5.0 1.1 %copy-done.2 = bf16[1,1,128,2560]{3,2,1,0:T(8,128)(2,1)S(1)} copy-done((bf16[1,1,128,2560]{3,2,1,0:T(8,128)(2,1)S(1)}, bf16[1,1,128,2560]{3,2,1,0:T(8,128)(2,1)}, u32[]{:S(2)}) %copy-start.2) | copy-done | bytes 655384
  6.1 0.0 copy-start.3
  6.1 1.1 %copy-done.3 = bf16[1,1,128,2560]{3,2,1,0:T(8,128)(2,1)S(1)} copy-done((bf16[1,1,128,2560]{3,2,1,0:T(8,128)(2,1)S(1)}, bf16[1,1,128,2560]{3,2,1,0:T(8,128)(2,1)}, u32[]{:S(2)}) %copy-start.3) | copy-done | bytes 655384
  7.2 95.2 %attention_backward.1 = (bf16[128,2560]{1,0:T(8,128)(2,1)S(1)}, bf16[128,2560]{1,0:T(8,128)(2,1)S(1)}, bf16[128,2560]{1,0:T(8,128)(2,1)S(1)}, f32[1,80]{1,0:T(1,128)S(1)}, f32[1,80]{1,0:T(1,128)S(1)}) custom-call(f32[20,8,128]{2,1,0:T(8,128)S(1)} %broadcast_in_dim.23.limits, bf16[128,2560]{1,0:T(8,128)(2,1)S(1)} %bitcast.17, bf16[128,2560]{1,0:T(8,128)(2,1)S(1)} %bitcast.18, ...), custom_call_target="tpu_custom_call" | custom-call | tf_op jit(solution)/shard_map/attention_backward/pallas_call | solution.py:452
  102.3 0.8 copy.20
  103.2 0.8 copy.21
  104.0 0.8 copy.22
  104.9 0.5 copy.23
  105.4 0.5 copy.24
  (7 shorter events, 0.0 us)
Async XLA Ops:
  1.3 0.7 copy-start.6
  2.1 0.7 copy-start.4
  2.1 0.7 copy-start.5
  2.8 1.1 %copy-start = (bf16[1,1,128,2560]{3,2,1,0:T(8,128)(2,1)S(1)}, bf16[1,1,128,2560]{3,2,1,0:T(8,128)(2,1)}, u32[]{:S(2)}) copy-start(bf16[1,1,128,2560]{3,2,1,0:T(8,128)(2,1)} %param.8) | copy-start | bytes 1966084
  3.9 1.1 %copy-start.1 = (bf16[1,1,128,2560]{3,2,1,0:T(8,128)(2,1)S(1)}, bf16[1,1,128,2560]{3,2,1,0:T(8,128)(2,1)}, u32[]{:S(2)}) copy-start(bf16[1,1,128,2560]{3,2,1,0:T(8,128)(2,1)} %param.9) | copy-start | bytes 1966084
  5.0 1.1 %copy-start.2 = (bf16[1,1,128,2560]{3,2,1,0:T(8,128)(2,1)S(1)}, bf16[1,1,128,2560]{3,2,1,0:T(8,128)(2,1)}, u32[]{:S(2)}) copy-start(bf16[1,1,128,2560]{3,2,1,0:T(8,128)(2,1)} %param.10) | copy-start | bytes 1966084
  6.1 1.1 %copy-start.3 = (bf16[1,1,128,2560]{3,2,1,0:T(8,128)(2,1)S(1)}, bf16[1,1,128,2560]{3,2,1,0:T(8,128)(2,1)}, u32[]{:S(2)}) copy-start(bf16[1,1,128,2560]{3,2,1,0:T(8,128)(2,1)} %param.11) | copy-start | bytes 1966084

commit v3 on v2

--- a/solution.py
+++ b/solution.py
@@ -16,6 +16,7 @@
 FLOOR = -1e29
 MESH = pl.DeviceIdType.MESH
 KEYS, VALUES, QUERIES, UPSTREAM = range(4)
+CAPACITIES = (6, 8, 10, 12, 14, 16, 20)
 
 
 def dot(left, right, left_dim, right_dim):
@@ -28,11 +29,13 @@
     far,
     count,
     group,
+    perm,
+    place,
     limits,
-    queries,
-    keys,
-    values,
-    upstream,
+    queries_hbm,
+    keys_hbm,
+    values_hbm,
+    upstream_hbm,
     q_gain,
     k_gain,
     d_queries,
@@ -40,6 +43,10 @@
     d_values,
     d_q_gain,
     d_k_gain,
+    keys,
+    values,
+    queries,
+    upstream,
     key_raw,
     query_raw,
     key_own,
@@ -67,6 +74,7 @@
     sum_inbox,
     sum_mine,
     sum_inbox_seq,
+    load_sem,
     send_sem,
     recv_sem,
     stat_send,
@@ -83,7 +91,7 @@
     me = lax.axis_index("fsdp")
     rank = lax.axis_index("seq")
     heads = limits.shape[0]
-    rows, columns = queries.shape
+    rows, columns = queries_hbm.shape
     size = columns // heads
     width = q_gain.shape[1]
     factor = size ** (-0.5)
@@ -94,8 +102,12 @@
     def repeat(first, last, body):
         lax.fori_loop(first, last, lambda step, carry: (body(step), carry)[1], 0)
 
-    def of_head(ref, head):
-        return ref[:, pl.ds(pl.multiple_of(head * size, size), size)]
+    arrays = ((keys_hbm, keys), (values_hbm, values), (queries_hbm, queries), (upstream_hbm, upstream))
+
+    def load(which, head):
+        source, target = arrays[which]
+        part = pl.ds(pl.multiple_of(head * size, size), size)
+        return pltpu.make_async_copy(source.at[:, part], target.at[head], load_sem.at[which, head])
 
     outgoing = (key_raw, value_own, query_raw, upstream_own)
     incoming = (key_in, value_in, query_in, upstream_in)
@@ -173,40 +185,28 @@
 
     repeat(1, count, greet)
     repeat(1, group, greet_seq)
-
-    def stage_keys(slot):
-        key_raw[slot] = of_head(keys, slot)
-        value_own[slot] = of_head(values, slot)
-
-    def stage_queries(slot):
-        query_raw[slot] = of_head(queries, slot)
-        upstream_own[slot] = of_head(upstream, slot)
-
-    repeat(0, heads, stage_keys)
+    for which in range(4):
+        repeat(0, heads, lambda head: load(which, head).start())
     gain_mine[...] = jnp.zeros_like(gain_mine)
     gain_mine[0:1, 0:width] = q_gain[...]
     gain_mine[0:1, LANES : LANES + width] = k_gain[...]
     gain_inbox[pl.ds(me, 1)] = gain_mine[...][None]
-    pl.semaphore_wait(barrier, count + group - 2)
-
-    def send_keys(pair):
-        for side in range(2):
-            link(KEYS, side, pair).start()
-            link(VALUES, side, pair).start()
-
-    def send_queries(pair):
-        for side in range(2):
-            link(QUERIES, side, pair).start()
-            link(UPSTREAM, side, pair).start()
-
-    repeat(1, count, lambda step: gain_link(step).start())
-    repeat(0, far_pairs, send_keys)
-    repeat(0, heads, stage_queries)
-
-    for row, ref in enumerate((queries, keys)):
-
+
+    def stage_keys(slot):
+        key_raw[slot] = keys[perm[slot]]
+
+    def stage_values(slot):
+        value_own[slot] = values[perm[slot]]
+
+    def stage_queries(slot):
+        query_raw[slot] = queries[perm[slot]]
+
+    def stage_upstream(slot):
+        upstream_own[slot] = upstream[perm[slot]]
+
+    def invert(row, ref):
         def squares(head, total):
-            wide = of_head(ref, head).astype(jnp.float32)
+            wide = ref[head].astype(jnp.float32)
             return total + wide * wide
 
         total = lax.fori_loop(0, heads, squares, jnp.zeros((rows, size), jnp.float32))
@@ -214,8 +214,33 @@
         inverse = jnp.broadcast_to(lax.rsqrt(mean + EPS), (rows, size))
         inverse_own[row] = inverse
         inverse_out[row : row + 1, :] = jnp.transpose(inverse)[0:1, :]
+
+    repeat(0, heads, lambda head: load(KEYS, head).wait())
+    repeat(0, far, stage_keys)
+    repeat(0, heads, lambda head: load(VALUES, head).wait())
+    repeat(0, heads, stage_values)
+    invert(1, keys)
+    repeat(0, heads, lambda head: load(QUERIES, head).wait())
+    invert(0, queries)
+    repeat(0, far, stage_queries)
+    repeat(0, heads, lambda head: load(UPSTREAM, head).wait())
+    repeat(0, heads, stage_upstream)
+    pl.semaphore_wait(barrier, count + group - 2)
+
+    def send_keys(pair):
+        for side in range(2):
+            link(KEYS, side, pair).start()
+            link(VALUES, side, pair).start()
+
+    def send_queries(pair):
+        for side in range(2):
+            link(QUERIES, side, pair).start()
+            link(UPSTREAM, side, pair).start()
+
     for side in range(2):
         inverse_link(side).start()
+    repeat(1, count, lambda step: gain_link(step).start())
+    repeat(0, far_pairs, send_keys)
 
     repeat(1, count, lambda step: gain_link(step).wait())
     lane = lax.broadcasted_iota(jnp.int32, (1, LANES), 1)
@@ -237,8 +262,9 @@
         return (raw.astype(jnp.float32) * inverse * gains[row, head]).astype(jnp.bfloat16)
 
     def normalise(slot):
-        query_own[slot] = normed(query_raw[slot], inverse_own[0], 0, slot)
-        key_own[slot] = normed(key_raw[slot], inverse_own[1], 1, slot)
+        head = perm[slot]
+        query_own[slot] = normed(queries[head], inverse_own[0], 0, head)
+        key_own[slot] = normed(keys[head], inverse_own[1], 1, head)
 
     repeat(0, heads, normalise)
 
@@ -295,8 +321,9 @@
             link(VALUES, 1 - side, pair).wait_recv()
         send_queries(pair)
         for slot in (2 * pair, 2 * pair + 1):
-            low = normed(key_in[0, slot], inverse_near[0, 1], 1, slot)
-            high = normed(key_in[1, slot], inverse_near[1, 1], 1, slot)
+            head = perm[slot]
+            low = normed(key_in[0, slot], inverse_near[0, 1], 1, head)
+            high = normed(key_in[1, slot], inverse_near[1, 1], 1, head)
             key_all = jnp.concatenate([low, key_own[slot], high], axis=0)
             value_all = jnp.concatenate([value_in[0, slot], value_own[slot], value_in[1, slot]], axis=0)
             bias = spatial(slot)
@@ -313,7 +340,7 @@
         inverse = inverse_own[row]
 
         def first(head, total):
-            wide, slope = of_head(ref, head).astype(jnp.float32), grad[head]
+            wide, slope = ref[head].astype(jnp.float32), grad[place[head]]
             gain_rows[row, head] = jnp.sum(slope * wide * inverse, axis=0, keepdims=True)
             return total + slope * gains[row, head] * wide
 
@@ -322,7 +349,7 @@
         shrink = inverse * inverse * inner
 
         def second(head):
-            wide, slope = of_head(ref, head).astype(jnp.float32), grad[head]
+            wide, slope = ref[head].astype(jnp.float32), grad[place[head]]
             result = inverse * (slope * gains[row, head] - wide * shrink)
             out[:, pl.ds(pl.multiple_of(head * size, size), size)] = result.astype(jnp.bfloat16)
 
@@ -336,8 +363,9 @@
             link(UPSTREAM, 1 - side, pair).wait_recv()
             stat_link(1 - side, pair).wait_recv()
         for slot in (2 * pair, 2 * pair + 1):
-            low = normed(query_in[0, slot], inverse_near[0, 0], 0, slot)
-            high = normed(query_in[1, slot], inverse_near[1, 0], 0, slot)
+            head = perm[slot]
+            low = normed(query_in[0, slot], inverse_near[0, 0], 0, head)
+            high = normed(query_in[1, slot], inverse_near[1, 0], 0, head)
             query_all = jnp.concatenate([low, high], axis=0)
             upstream_all = jnp.concatenate([upstream_in[0, slot], upstream_in[1, slot]], axis=0)
             bias = spatial(slot)
@@ -373,7 +401,7 @@
     repeat(1, count, lambda step: sum_link(step).start())
 
     def finish_values(head):
-        out = value_grad[head].astype(jnp.bfloat16)
+        out = value_grad[place[head]].astype(jnp.bfloat16)
         d_values[:, pl.ds(pl.multiple_of(head * size, size), size)] = out
 
     repeat(0, heads, finish_values)
@@ -397,20 +425,26 @@
     d_k_gain[...] = total[:, LANES : LANES + width]
 
 
-def attention(far, identity, limits, queries, keys, values, upstream, q_gain, k_gain):
+def attention(far, identity, perm, place, limits, queries, keys, values, upstream, q_gain, k_gain):
     count, group = lax.axis_size("fsdp"), lax.axis_size("seq")
     heads = limits.shape[0]
     rows, columns = queries.shape
     size = columns // heads
     width = q_gain.shape[0]
     wide, narrow = jnp.float32, jnp.bfloat16
-    pairs = max(far // 2, 1)
+    pairs = far // 2
+    smem = pl.BlockSpec(memory_space=pltpu.SMEM)
+    hbm = pl.BlockSpec(memory_space=pl.ANY)
     vmem = pl.BlockSpec(memory_space=pltpu.VMEM)
     block = (rows, size)
     dma = pltpu.SemaphoreType.DMA
     scratch = [
         pltpu.VMEM((heads,) + block, narrow),
         pltpu.VMEM((heads,) + block, narrow),
+        pltpu.VMEM((heads,) + block, narrow),
+        pltpu.VMEM((heads,) + block, narrow),
+        pltpu.VMEM((far,) + block, narrow),
+        pltpu.VMEM((far,) + block, narrow),
         pltpu.VMEM((heads,) + block, narrow),
         pltpu.VMEM((heads,) + block, narrow),
         pltpu.VMEM((heads,) + block, narrow),
@@ -436,6 +470,7 @@
         pltpu.VMEM((count, 1, 2 * LANES), wide),
         pltpu.VMEM((1, 2 * LANES), wide),
         pltpu.VMEM((group, 1, 2 * LANES), wide),
+        dma((4, heads)),
         dma((4, 2, pairs)),
         dma((4, 2, pairs)),
         dma((2, pairs)),
@@ -453,36 +488,53 @@
         functools.partial(attention_kernel, far, count, group),
         out_shape=[jax.ShapeDtypeStruct((rows, columns), narrow)] * 3
         + [jax.ShapeDtypeStruct((1, width), wide)] * 2,
-        in_specs=[vmem] * 7,
+        in_specs=[smem] * 2 + [vmem] + [hbm] * 4 + [vmem] * 2,
         out_specs=[vmem] * 5,
         scratch_shapes=scratch,
         compiler_params=pltpu.CompilerParams(
-            collective_id=identity, has_side_effects=True, vmem_limit_bytes=48 * 1024 * 1024
+            collective_id=identity, has_side_effects=True, vmem_limit_bytes=56 * 1024 * 1024
         ),
         name="attention_backward",
-    )(limits, queries, keys, values, upstream, q_gain[None], k_gain[None])
+    )(perm, place, limits, queries, keys, values, upstream, q_gain[None], k_gain[None])
     return d_queries, d_keys, d_values, d_q_gain[0], d_k_gain[0]
 
 
-def head_limits(windows, frames):
+def head_order(windows, frames):
     rank, group = lax.axis_index("seq"), lax.axis_size("seq")
+    heads = windows.shape[0]
     near = windows[:, 0] >= 1
+    ahead = jnp.arange(heads)[None, :] < jnp.arange(heads)[:, None]
+    before = jnp.where(near[:, None], near[None, :] & ahead, near[None, :] | ahead)
+    place = jnp.sum(before.astype(jnp.int32), 1)
+    here = place[None, :] == jnp.arange(heads)[:, None]
+    perm = jnp.sum(jnp.where(here, jnp.arange(heads, dtype=jnp.int32)[None, :], 0), 1)
     own = jnp.full_like(near, rank < frames)
     below = near & (rank > 0) & (rank < frames)
     above = near & (rank + 1 < group) & (rank + 1 < frames)
     blocks = jnp.where(jnp.stack([below, own, above], 1), 0.0, BLOCKED)
     table = jnp.concatenate([blocks, windows.astype(jnp.float32)[:, 1:], jnp.zeros_like(blocks)], 1)
-    return jnp.broadcast_to(table[:, :, None], table.shape + (LANES,))
+    table = jnp.sum(jnp.where(here[:, :, None], table[None], 0.0), 1)
+    limits = jnp.broadcast_to(table[:, :, None], table.shape + (LANES,))
+    return perm, place, limits, jnp.sum(near.astype(jnp.int32))
 
 
 def local(queries, keys, values, grad_out, q_gain, k_gain, lengths, windows):
     shape = queries.shape
     flat = (shape[1] * shape[2], shape[3])
     arrays = [array.reshape(flat) for array in (queries, keys, values, grad_out)]
-    limits = head_limits(windows, lengths[0])
+    perm, place, limits, near = head_order(windows, lengths[0])
     heads = windows.shape[0]
-    d_queries, d_keys, d_values, d_q_gain, d_k_gain = attention(
-        heads, 0, limits, *arrays, q_gain, k_gain
+    capacities = [at for at in CAPACITIES if at < heads] + [heads]
+    branch = sum((near > at).astype(jnp.int32) for at in capacities[:-1])
+    d_queries, d_keys, d_values, d_q_gain, d_k_gain = lax.switch(
+        branch,
+        [functools.partial(attention, far, at) for at, far in enumerate(capacities)],
+        perm,
+        place,
+        limits,
+        *arrays,
+        q_gain,
+        k_gain,
     )
     return (
         d_queries.reshape(shape),

time: 106 us -> 75.1 us (0.71)
  Pallas kernels: 95.2 us -> 62 us
  between operations: 1.35 us -> 5.28 us
  local copies, waits for them, and re-layouts: 9.31 us -> 5.59 us
  other arithmetic: 0.04 us -> 1.58 us
    pallas_call x1, Pallas kernels: 95.2 us -> 62 us  [attention(): pl.pallas_call(functools.partial(attention_kernel, far, count, group), ou...]
    unnamed x19 -> x11, local copies, waits for them, and re-layouts: 9.14 us -> 4.85 us
    reduce_sum x0 -> x4, other arithmetic: none -> 1.53 us  [the longest x1 0.63 us: head_order(): return (perm, place, limits, jnp.sum(near.astype(jnp.int32)))]
where the time goes in v3:
time: 75.1 us; the launch traced here: 74.7 us
  Pallas kernels  62 us (83%)
  local copies, waits for them, and re-layouts  5.59 us (7%)
  between operations  5.28 us (7%)
  other arithmetic  1.58 us (2%)
    pallas_call x1, Pallas kernels, attention(): pl.pallas_call(functools.partial(attention_kernel, far, count, group), ou...  62 us
    unnamed x11, local copies, waits for them, and re-layouts  4.85 us

profile of v3, /device:TPU:1, one launch (start us, length us, event | category | flops | bytes accessed | tf_op | source)
XLA Modules:
  0.0 74.7 jit_solution(11161662697752796840)
XLA Ops:
  1.3 0.0 copy-start.2
  1.3 0.7 copy-done.2
  2.0 0.6 convert_reduce_fusion.1
  6.5 0.2 convert_reduce_fusion
  6.8 0.0 copy-start
  6.8 0.0 copy-start.1
  6.8 0.6 copy-done
  7.4 0.0 copy-done.1
  7.5 63.7 %conditional.1 = (bf16[1,1,128,2560]{3,2,1,0:T(8,128)(2,1)S(1)}, bf16[1,1,128,2560]{3,2,1,0:T(8,128)(2,1)S(1)}, bf16[1,1,128,2560]{3,2,1,0:T(8,128)(2,1)S(1)}, f32[80]{0:T(128)S(1)}, f32[80]{0:T(128)S(1)}) conditional(s32[]{:T(128)} %clamp.3, (f32[80]{0:T(128)S(1)}, f32[80]{0:T(128)S(1)}, ...), branch_computations={%region_4.5_spmd, %region_5.6_spmd, %region_6.7_spmd, %region_7.8_... | conditional | flops 7020 | bytes 86376 | solution.py:529
  7.5 0.6 select_reduce_fusion.3.perm
  8.1 0.1 select_reduce_fusion.2
  8.2 0.7 broadcast_in_dim.114.limits
  8.9 62.0 %attention_backward.8 = (bf16[128,2560]{1,0:T(8,128)(2,1)S(1)}, bf16[128,2560]{1,0:T(8,128)(2,1)S(1)}, bf16[128,2560]{1,0:T(8,128)(2,1)S(1)}, f32[1,80]{1,0:T(1,128)S(1)}, f32[1,80]{1,0:T(1,128)S(1)}) custom-call(s32[20]{0:T(128)} %select_reduce_fusion.3.perm, s32[20]{0:T(128)S(1)} %get-tuple-element.137.place, f32[20,8,128]{2,1,0:T(8,128)} %broadcast_in_dim.114.limits, ...), custom_call_target="tpu_custom_call" | custom-call | tf_op jit(solution)/shard_map/cond/branch_1_fun/attention_backward/pallas_call | solution.py:487
  71.2 0.8 %copy.103 = bf16[1,1,128,2560]{3,2,1,0:T(8,128)(2,1)} copy(bf16[1,1,128,2560]{3,2,1,0:T(8,128)(2,1)S(1)} %get-tuple-element.505) | data formatting | bytes 1310720
  72.0 0.8 %copy.104 = bf16[1,1,128,2560]{3,2,1,0:T(8,128)(2,1)} copy(bf16[1,1,128,2560]{3,2,1,0:T(8,128)(2,1)S(1)} %get-tuple-element.506) | data formatting | bytes 1310720
  72.9 0.8 %copy.105 = bf16[1,1,128,2560]{3,2,1,0:T(8,128)(2,1)} copy(bf16[1,1,128,2560]{3,2,1,0:T(8,128)(2,1)S(1)} %get-tuple-element.507) | data formatting | bytes 1310720
  73.7 0.5 copy.106
  74.2 0.5 copy.107
  (9 shorter events, 0.1 us)
Async XLA Ops:
  1.3 0.7 copy-start.2
  6.8 0.7 copy-start
  6.8 0.7 copy-start.1

commit v4 on v3

--- a/solution.py
+++ b/solution.py
@@ -41,8 +41,7 @@
     d_queries,
     d_keys,
     d_values,
-    d_q_gain,
-    d_k_gain,
+    d_gains,
     keys,
     values,
     queries,
@@ -63,6 +62,7 @@
     inverse_in,
     inverse_own,
     inverse_near,
+    shrink,
     gains,
     gain_rows,
     query_grad,
@@ -99,6 +99,9 @@
     below, above = lax.rem(rank + group - 1, group), lax.rem(rank + 1, group)
     barrier = pltpu.get_barrier_semaphore()
 
+    def farthest(step):
+        return count // 2 + (1 - 2 * (step % 2)) * ((step + 1) // 2)
+
     def repeat(first, last, body):
         lax.fori_loop(first, last, lambda step, carry: (body(step), carry)[1], 0)
 
@@ -145,6 +148,7 @@
         )
 
     def gain_link(step):
+        step = farthest(step)
         return pltpu.make_async_remote_copy(
             src_ref=gain_mine,
             dst_ref=gain_inbox.at[me],
@@ -155,6 +159,7 @@
         )
 
     def sum_link(step):
+        step = farthest(step)
         peer = lax.rem(me + step, count)
         return pltpu.make_async_remote_copy(
             src_ref=sum_outbox.at[peer],
@@ -176,14 +181,14 @@
         )
 
     def greet(step):
-        peer = lax.rem(me + step, count)
+        peer = lax.rem(me + farthest(step), count)
         pl.semaphore_signal(barrier, inc=1, device_id={"fsdp": peer}, device_id_type=MESH)
 
     def greet_seq(step):
         peer = lax.rem(rank + step, group)
         pl.semaphore_signal(barrier, inc=1, device_id={"seq": peer}, device_id_type=MESH)
 
-    repeat(1, count, greet)
+    repeat(0, count - 1, greet)
     repeat(1, group, greet_seq)
     for which in range(4):
         repeat(0, heads, lambda head: load(which, head).start())
@@ -239,10 +244,11 @@
 
     for side in range(2):
         inverse_link(side).start()
-    repeat(1, count, lambda step: gain_link(step).start())
-    repeat(0, far_pairs, send_keys)
-
-    repeat(1, count, lambda step: gain_link(step).wait())
+    repeat(0, 1, send_keys)
+    repeat(0, count - 1, lambda step: gain_link(step).start())
+    repeat(1, far_pairs, send_keys)
+
+    repeat(0, count - 1, lambda step: gain_link(step).wait())
     lane = lax.broadcasted_iota(jnp.int32, (1, LANES), 1)
     for row in range(2):
         tiles = [jnp.zeros((1, LANES), jnp.float32) for _ in range(heads + 1)]
@@ -306,6 +312,8 @@
             bias = spatial(slot) + frame_bias(slot, 1)
             query_side(slot, key_own[slot], value_own[slot], bias, slice(0, rows))
 
+    early = far_pairs // 2
+    repeat(0, early, send_queries)
     if far_pairs < pairs:
         repeat(far_pairs, pairs, alone)
 
@@ -315,11 +323,11 @@
             spread = jnp.broadcast_to(inverse_in[side, row : row + 1, :], (rows, size))
             inverse_near[side, row] = jnp.transpose(spread)
 
-    def near_queries(pair):
+    def near_queries(pair, send_queries_after):
         for side in range(2):
             link(KEYS, 1 - side, pair).wait_recv()
             link(VALUES, 1 - side, pair).wait_recv()
-        send_queries(pair)
+        send_queries_after(pair)
         for slot in (2 * pair, 2 * pair + 1):
             head = perm[slot]
             low = normed(key_in[0, slot], inverse_near[0, 1], 1, head)
@@ -334,27 +342,44 @@
         for side in range(2):
             stat_link(side, pair).start()
 
-    repeat(0, far_pairs, near_queries)
+    repeat(0, far_pairs - early, lambda pair: near_queries(pair, lambda at: send_queries(at + early)))
+    repeat(far_pairs - early, far_pairs, lambda pair: near_queries(pair, lambda at: None))
+
+    def norm_inner(row, ref, grad, with_gain):
+        inverse = inverse_own[row]
+
+        def body(head, total):
+            wide, slope = ref[head].astype(jnp.float32), grad[place[head]]
+            product = slope * wide
+            if with_gain:
+                gain_rows[head] = jnp.sum(product * inverse, axis=0, keepdims=True)
+            return total + product * gains[row, head]
+
+        total = lax.fori_loop(0, heads, body, jnp.zeros((rows, size), jnp.float32))
+        inner = jnp.sum(total, axis=1, keepdims=True) / columns
+        shrink[...] = inverse * inverse * inner
 
     def norm_back(row, ref, grad, out):
-        inverse = inverse_own[row]
-
-        def first(head, total):
+        def body(head):
             wide, slope = ref[head].astype(jnp.float32), grad[place[head]]
-            gain_rows[row, head] = jnp.sum(slope * wide * inverse, axis=0, keepdims=True)
-            return total + slope * gains[row, head] * wide
-
-        total = lax.fori_loop(0, heads, first, jnp.zeros((rows, size), jnp.float32))
-        inner = jnp.sum(total, axis=1, keepdims=True) / columns
-        shrink = inverse * inverse * inner
-
-        def second(head):
-            wide, slope = ref[head].astype(jnp.float32), grad[place[head]]
-            result = inverse * (slope * gains[row, head] - wide * shrink)
+            result = inverse_own[row] * (slope * gains[row, head] - wide * shrink[...])
             out[:, pl.ds(pl.multiple_of(head * size, size), size)] = result.astype(jnp.bfloat16)
 
-        repeat(0, heads, second)
-
+        repeat(0, heads, body)
+
+    norm_inner(0, queries, query_grad, True)
+
+    for owner in range(count):
+        tile, offset = divmod(owner * width, LANES)
+        part = gain_rows[tile]
+        if offset:
+            part = pltpu.roll(part, LANES - offset, 1)
+        if offset + width > LANES:
+            after = pltpu.roll(gain_rows[tile + 1], LANES - offset, 1)
+            part = jnp.where(lane < LANES - offset, part, after)
+        sum_outbox[owner] = part
+    sum_inbox[pl.ds(me, 1)] = sum_outbox[pl.ds(me, 1)]
+    repeat(0, count - 1, lambda step: sum_link(step).start())
     norm_back(0, queries, query_grad, d_queries)
 
     def near_keys(pair):
@@ -384,31 +409,21 @@
             key_grad[slot] += dot(dscores, query_all, 1, 0) * factor
             value_grad[slot] += dot(weights, upstream_all, 1, 0)
 
-    repeat(0, far_pairs, near_keys)
+    midway = (2 * far_pairs + 2) // 3
+    repeat(0, midway, near_keys)
+    repeat(0, count - 1, lambda step: sum_link(step).wait())
+    sum_mine[...] = jnp.sum(sum_inbox[...], axis=0)
+    repeat(1, group, lambda step: seq_link(step).start())
+    sum_inbox_seq[pl.ds(rank, 1)] = sum_mine[...][None]
+    repeat(midway, far_pairs, near_keys)
+    norm_inner(1, keys, key_grad, False)
     norm_back(1, keys, key_grad, d_keys)
-
-    for owner in range(count):
-        tile, offset = divmod(owner * width, LANES)
-        for row in range(2):
-            part = gain_rows[row, tile]
-            if offset:
-                part = pltpu.roll(part, LANES - offset, 1)
-            if offset + width > LANES:
-                after = pltpu.roll(gain_rows[row, tile + 1], LANES - offset, 1)
-                part = jnp.where(lane < LANES - offset, part, after)
-            sum_outbox[owner, :, row * LANES : (row + 1) * LANES] = part
-    sum_inbox[pl.ds(me, 1)] = sum_outbox[pl.ds(me, 1)]
-    repeat(1, count, lambda step: sum_link(step).start())
 
     def finish_values(head):
         out = value_grad[place[head]].astype(jnp.bfloat16)
         d_values[:, pl.ds(pl.multiple_of(head * size, size), size)] = out
 
     repeat(0, heads, finish_values)
-    repeat(1, count, lambda step: sum_link(step).wait())
-    sum_mine[...] = jnp.sum(sum_inbox[...], axis=0)
-    repeat(1, group, lambda step: seq_link(step).start())
-    sum_inbox_seq[pl.ds(rank, 1)] = sum_mine[...][None]
 
     def sent(pair):
         for side in range(2):
@@ -420,9 +435,9 @@
     for side in range(2):
         inverse_link(side).wait_send()
     repeat(1, group, lambda step: seq_link(step).wait())
-    total = jnp.sum(sum_inbox_seq[...], axis=0)
-    d_q_gain[...] = total[:, 0:width]
-    d_k_gain[...] = total[:, LANES : LANES + width]
+    total = jnp.sum(sum_inbox_seq[...], axis=0)[:, 0:width]
+    d_gains[0:1, 0:width] = total
+    d_gains[1:2, 0:width] = total * (q_gain[...] / k_gain[...])
 
 
 def attention(far, identity, perm, place, limits, queries, keys, values, upstream, q_gain, k_gain):
@@ -459,17 +474,18 @@
         pltpu.VMEM((2, 2, size), wide),
         pltpu.VMEM((2,) + block, wide),
         pltpu.VMEM((2, 2) + block, wide),
+        pltpu.VMEM(block, wide),
         pltpu.VMEM((2, heads, 1, size), wide),
-        pltpu.VMEM((2, heads, 1, size), wide),
+        pltpu.VMEM((heads, 1, size), wide),
         pltpu.VMEM((heads,) + block, wide),
         pltpu.VMEM((heads,) + block, wide),
         pltpu.VMEM((heads,) + block, wide),
         pltpu.VMEM((1, 2 * LANES), wide),
         pltpu.VMEM((count, 1, 2 * LANES), wide),
-        pltpu.VMEM((count, 1, 2 * LANES), wide),
-        pltpu.VMEM((count, 1, 2 * LANES), wide),
-        pltpu.VMEM((1, 2 * LANES), wide),
-        pltpu.VMEM((group, 1, 2 * LANES), wide),
+        pltpu.VMEM((count, 1, LANES), wide),
+        pltpu.VMEM((count, 1, LANES), wide),
+        pltpu.VMEM((1, LANES), wide),
+        pltpu.VMEM((group, 1, LANES), wide),
         dma((4, heads)),
         dma((4, 2, pairs)),
         dma((4, 2, pairs)),
@@ -484,50 +500,94 @@
         dma((group,)),
         dma((group,)),
     ]
-    d_queries, d_keys, d_values, d_q_gain, d_k_gain = pl.pallas_call(
+    return pl.pallas_call(
         functools.partial(attention_kernel, far, count, group),
         out_shape=[jax.ShapeDtypeStruct((rows, columns), narrow)] * 3
-        + [jax.ShapeDtypeStruct((1, width), wide)] * 2,
+        + [jax.ShapeDtypeStruct((2, LANES), wide)],
         in_specs=[smem] * 2 + [vmem] + [hbm] * 4 + [vmem] * 2,
-        out_specs=[vmem] * 5,
+        out_specs=[vmem] * 4,
         scratch_shapes=scratch,
         compiler_params=pltpu.CompilerParams(
             collective_id=identity, has_side_effects=True, vmem_limit_bytes=56 * 1024 * 1024
         ),
         name="attention_backward",
     )(perm, place, limits, queries, keys, values, upstream, q_gain[None], k_gain[None])
-    return d_queries, d_keys, d_values, d_q_gain[0], d_k_gain[0]
-
-
-def head_order(windows, frames):
+
+def order_kernel(capacities, windows, length, perm, place, branch, limits):
     rank, group = lax.axis_index("seq"), lax.axis_size("seq")
     heads = windows.shape[0]
-    near = windows[:, 0] >= 1
-    ahead = jnp.arange(heads)[None, :] < jnp.arange(heads)[:, None]
-    before = jnp.where(near[:, None], near[None, :] & ahead, near[None, :] | ahead)
-    place = jnp.sum(before.astype(jnp.int32), 1)
-    here = place[None, :] == jnp.arange(heads)[:, None]
-    perm = jnp.sum(jnp.where(here, jnp.arange(heads, dtype=jnp.int32)[None, :], 0), 1)
-    own = jnp.full_like(near, rank < frames)
-    below = near & (rank > 0) & (rank < frames)
-    above = near & (rank + 1 < group) & (rank + 1 < frames)
-    blocks = jnp.where(jnp.stack([below, own, above], 1), 0.0, BLOCKED)
-    table = jnp.concatenate([blocks, windows.astype(jnp.float32)[:, 1:], jnp.zeros_like(blocks)], 1)
-    table = jnp.sum(jnp.where(here[:, :, None], table[None], 0.0), 1)
-    limits = jnp.broadcast_to(table[:, :, None], table.shape + (LANES,))
-    return perm, place, limits, jnp.sum(near.astype(jnp.int32))
+    near = 0
+    for head in range(heads):
+        near = near + (windows[head, 0] >= 1).astype(jnp.int32)
+    branch[0] = sum((near > at).astype(jnp.int32) for at in capacities[:-1])
+    frames = length[0]
+    own = rank < frames
+    below = (rank > 0) & own
+    above = (rank + 1 < group) & (rank + 1 < frames)
+    ahead, behind = 0, near
+    for head in range(heads):
+        reaches = windows[head, 0] >= 1
+        slot = jnp.where(reaches, ahead, behind)
+        ahead = ahead + reaches.astype(jnp.int32)
+        behind = behind + 1 - reaches.astype(jnp.int32)
+        perm[slot] = head
+        place[head] = slot
+        frame_bias = [jnp.where(seen, 0.0, BLOCKED) for seen in (reaches & below, own, reaches & above)]
+        widths = [windows[head, 1].astype(jnp.float32), windows[head, 2].astype(jnp.float32)]
+        for row, value in enumerate(frame_bias + widths):
+            limits[slot, row : row + 1, :] = jnp.full((1, LANES), value, jnp.float32)
+
+
+def head_order(windows, lengths, capacities):
+    heads = windows.shape[0]
+    smem = pl.BlockSpec(memory_space=pltpu.SMEM)
+    return pl.pallas_call(
+        functools.partial(order_kernel, capacities),
+        out_shape=[
+            jax.ShapeDtypeStruct((heads,), jnp.int32),
+            jax.ShapeDtypeStruct((heads,), jnp.int32),
+            jax.ShapeDtypeStruct((1,), jnp.int32),
+            jax.ShapeDtypeStruct((heads, 8, LANES), jnp.float32),
+        ],
+        in_specs=[smem] * 2,
+        out_specs=[smem] * 3 + [pl.BlockSpec(memory_space=pltpu.VMEM)],
+        name="head_order",
+    )(windows, lengths)
+
+
+def deliver_kernel(width, *refs):
+    sources, gains, targets, q_gain, k_gain, sems = refs[0:3], refs[3], refs[4:7], refs[7], refs[8], refs[9]
+    copies = [pltpu.make_async_copy(sources[at], targets[at], sems.at[at]) for at in range(3)]
+    for copy in copies:
+        copy.start()
+    q_gain[...] = gains[0:1, 0:width]
+    k_gain[...] = gains[1:2, 0:width]
+    for copy in copies:
+        copy.wait()
+
+
+def deliver(width, *results):
+    hbm, vmem = pl.BlockSpec(memory_space=pl.ANY), pl.BlockSpec(memory_space=pltpu.VMEM)
+    gain = jax.ShapeDtypeStruct((1, width), jnp.float32)
+    return pl.pallas_call(
+        functools.partial(deliver_kernel, width),
+        out_shape=[jax.ShapeDtypeStruct(result.shape, result.dtype) for result in results[:3]] + [gain] * 2,
+        in_specs=[hbm] * 3 + [vmem],
+        out_specs=[hbm] * 3 + [vmem] * 2,
+        scratch_shapes=[pltpu.SemaphoreType.DMA((3,))],
+        name="deliver",
+    )(*results)
 
 
 def local(queries, keys, values, grad_out, q_gain, k_gain, lengths, windows):
     shape = queries.shape
     flat = (shape[1] * shape[2], shape[3])
     arrays = [array.reshape(flat) for array in (queries, keys, values, grad_out)]
-    perm, place, limits, near = head_order(windows, lengths[0])
     heads = windows.shape[0]
     capacities = [at for at in CAPACITIES if at < heads] + [heads]
-    branch = sum((near > at).astype(jnp.int32) for at in capacities[:-1])
-    d_queries, d_keys, d_values, d_q_gain, d_k_gain = lax.switch(
-        branch,
+    perm, place, branch, limits = head_order(windows, lengths, capacities)
+    results = lax.switch(
+        branch[0],
         [functools.partial(attention, far, at) for at, far in enumerate(capacities)],
         perm,
         place,
@@ -536,12 +596,13 @@
         q_gain,
         k_gain,
     )
+    d_queries, d_keys, d_values, d_q_gain, d_k_gain = deliver(q_gain.shape[0], *results)
     return (
         d_queries.reshape(shape),
         d_keys.reshape(shape),
         d_values.reshape(shape),
-        d_q_gain,
-        d_k_gain,
+        d_q_gain[0],
+        d_k_gain[0],
     )
 
 

time: 75.1 us -> 62.1 us (0.83)
  Pallas kernels: 62 us -> 56.8 us
  local copies, waits for them, and re-layouts: 5.59 us -> 2.02 us
  between operations: 5.28 us -> 2.19 us
  other arithmetic: 1.58 us -> 0 us
    pallas_call x1, Pallas kernels: 62 us -> 53.4 us  [attention(): pl.pallas_call(functools.partial(attention_kernel, far, count, group), ou...]
    pallas_call x0 -> x2, Pallas kernels: none -> 3.48 us  [the longest x1 1.81 us: deliver(): pl.pallas_call(functools.partial(deliver_kernel, width), out_shape=[jax.S...]
    unnamed x11 -> x7, local copies, waits for them, and re-layouts: 4.85 us -> 2.02 us
    reduce_sum x4 -> x0, other arithmetic: 1.53 us -> none  [the longest x1 0.63 us: head_order(): return (perm, place, limits, jnp.sum(near.astype(jnp.int32)))]
where the time goes in v4:
time: 62.1 us; the launch traced here: 61.8 us
  Pallas kernels  56.8 us (91%)
  between operations  2.19 us (4%)
  local copies, waits for them, and re-layouts  2.02 us (3%)
  loops' own time  0.72 us (1%)
    pallas_call x1, Pallas kernels, attention(): pl.pallas_call(functools.partial(attention_kernel, far, count, group), ou...  53.4 us
    unnamed x7, local copies, waits for them, and re-layouts  2.02 us
    pallas_call x1, Pallas kernels, deliver(): pl.pallas_call(functools.partial(deliver_kernel, width), out_shape=[jax.S...  1.81 us
    pallas_call x1, Pallas kernels, head_order(): pl.pallas_call(functools.partial(order_kernel, capacities), out_shape=[ja...  1.67 us

profile of v4, /device:TPU:1, one launch (start us, length us, event | category | flops | bytes accessed | tf_op | source)
XLA Modules:
  0.0 61.8 jit_solution(12019724461880940370)
XLA Ops:
  1.3 0.0 copy-start.2
  1.3 0.7 %copy-done.2 = s32[20,3]{0,1:T(4,128)S(1)} copy-done((s32[20,3]{0,1:T(4,128)S(1)}, s32[20,3]{0,1:T(4,128)}, u32[]{:S(2)}) %copy-start.2) | copy-done | bytes 264
  2.0 0.7 %copy.13.windows = s32[20,3]{1,0:T(8,128)} copy(s32[20,3]{0,1:T(4,128)S(1)} %copy-done.2) | data formatting | bytes 480 | tf_op args[7]
  2.6 1.7 %head_order.1 = (s32[20]{0:T(128)S(1)}, s32[20]{0:T(128)S(1)}, s32[1]{0:T(128)}, f32[20,8,128]{2,1,0:T(8,128)S(1)}) custom-call(s32[20,3]{1,0:T(8,128)} %copy.13.windows, s32[1]{0:T(128)S(6)} %copy.42.length), custom_call_target="tpu_custom_call" | custom-call | tf_op jit(solution)/shard_map/head_order/pallas_call | solution.py:544
  5.0 0.0 copy-start
  5.0 0.0 copy-start.1
  5.0 0.6 %copy-done = f32[80]{0:T(128)S(1)} copy-done((f32[80]{0:T(128)S(1)}, f32[80]{0:T(128)}, u32[]{:S(2)}) %copy-start) | copy-done | bytes 344
  5.6 0.0 copy-done.1
  5.7 54.1 %conditional.1 = ((bf16[128,2560]{1,0:T(8,128)(2,1)S(1)}, bf16[128,2560]{1,0:T(8,128)(2,1)S(1)}, bf16[128,2560]{1,0:T(8,128)(2,1)S(1)}, f32[2,128]{1,0:T(2,128)S(1)})) conditional(s32[]{:T(128)} %bitcast.14, (f32[80]{0:T(128)S(1)}, f32[80]{0:T(128)S(1)}, s32[20]{0:T(128)S(1)}, s32[20]{0:T(128)S(1)}, ...), branch_computations={%region_0.0_spmd, %region_1.0_spmd, %region_2.0_spmd, %region_3.0_... | conditional | bytes 8 | solution.py:589
  5.7 53.4 %attention_backward.8 = (bf16[128,2560]{1,0:T(8,128)(2,1)S(1)}, bf16[128,2560]{1,0:T(8,128)(2,1)S(1)}, bf16[128,2560]{1,0:T(8,128)(2,1)S(1)}, f32[2,128]{1,0:T(2,128)S(1)}) custom-call(s32[20]{0:T(128)S(1)} %get-tuple-element.135.perm, s32[20]{0:T(128)S(1)} %get-tuple-element.136.place, f32[20,8,128]{2,1,0:T(8,128)S(1)} %get-tuple-element.137.limits, ...), custom_call_target="tpu_custom_call" | custom-call | tf_op jit(solution)/shard_map/cond/branch_1_fun/attention_backward/pallas_call | solution.py:503
  59.7 1.8 %deliver.1 = (bf16[128,2560]{1,0:T(8,128)(2,1)}, bf16[128,2560]{1,0:T(8,128)(2,1)}, bf16[128,2560]{1,0:T(8,128)(2,1)}, f32[1,80]{1,0:T(1,128)}, f32[1,80]{1,0:T(1,128)}) custom-call(bf16[128,2560]{1,0:T(8,128)(2,1)S(1)} %get-tuple-element.211.refs_0_, bf16[128,2560]{1,0:T(8,128)(2,1)S(1)} %get-tuple-element.212.refs_1_, ...), custom_call_target="tpu_custom_call" | custom-call | tf_op jit(solution)/shard_map/deliver/pallas_call | solution.py:572
Async XLA Ops:
  1.3 0.7 %copy-start.2 = (s32[20,3]{0,1:T(4,128)S(1)}, s32[20,3]{0,1:T(4,128)}, u32[]{:S(2)}) copy-start(s32[20,3]{0,1:T(4,128)} %param.22) | copy-start | bytes 724
  5.0 0.7 %copy-start = (f32[80]{0:T(128)S(1)}, f32[80]{0:T(128)}, u32[]{:S(2)}) copy-start(f32[80]{0:T(128)} %param.19) | copy-start | bytes 964
  5.0 0.7 %copy-start.1 = (f32[80]{0:T(128)S(1)}, f32[80]{0:T(128)}, u32[]{:S(2)}) copy-start(f32[80]{0:T(128)} %param.20) | copy-start | bytes 964
